TPU v7x, 512 devices: a whole 4x4x16 slice. The times are simulated.
512 devices in a mesh: bx: 32 (over z, x_lo), by: 16 (over y, x_hi, core).
Axes of the slice: x: 4 (x_hi: 2, x_lo: 2; x = x_hi * 2 + x_lo), y: 4, z: 16, core: 2. Of those that a mesh axis runs over, the one named last changes fastest.
Arguments:
- state: float32 [4, 8, 512, 4096], P(None, None, 'by', 'bx'), may hold values from -6 to 6
- level_count: int32 [512, 4096], P('by', 'bx'), may hold values from 0 to 8, as said below
- coriolis: float32 [512], P('by'), may hold values from -1.5 to 1.5
Outputs:
- updated: float32 [4, 8, 512, 4096], P(None, None, 'by', 'bx')
Inputs may be any that keep to these rules, and one draw needn't show every extreme that they name: `level_count`: row 511 is full depth everywhere; the southernmost rows are land; whole blocks of 32 x 128 cells below the top block row may be land.
All inputs are finite; a program needn't handle non-finite values.
Results may differ from a plain program's by a relative error of at most 0.00002.
Values sent between devices are 32-bit elements; how exact they have to be, the bound alone decides.
A program may use at most 64 MiB of HBM per device.

v0:
```python
import jax
import jax.numpy as jnp
from jax import lax
from jax.sharding import PartitionSpec as P

DT = 0.2
KAPPA = 0.5
VISC = 0.4


def padded(value, sides, width, wrap):
    for axis, dim in sides:
        devices, length = (lax.axis_size(axis), value.shape[dim])
        up = [(i, (i + 1) % devices) for i in range(devices if wrap else devices - 1)]
        down = [(j, i) for i, j in up]
        last = lax.slice_in_dim(value, length - width, length, axis=dim)
        initial = lax.slice_in_dim(value, 0, width, axis=dim)
        before = lax.ppermute(last, axis, up)
        after = lax.ppermute(initial, axis, down)
        value = jnp.concatenate([before, value, after], axis=dim)
    return value


def swapped(value, axis, apart):
    return lax.ppermute(value, axis, [(i, i ^ 1 << apart) for i in range(lax.axis_size(axis))])


def neighbours(extended):
    return (
        extended[..., 1:-1, 2:],
        extended[..., 1:-1, :-2],
        extended[..., 2:, 1:-1],
        extended[..., :-2, 1:-1],
        extended[..., 1:-1, 1:-1],
    )


def extend(stacked, sign_table, width):
    zonal_ext = padded(stacked, (("bx", 3),), width, True)
    full_ext = padded(zonal_ext, (("by", 2),), width, False)
    top_rows = zonal_ext[:, :, -width:, :]
    mirrored = top_rows
    for position in range(lax.axis_size("bx").bit_length() - 1):
        mirrored = swapped(mirrored, "bx", position)
    ghost_rows = mirrored[:, :, ::-1, ::-1] * sign_table
    on_top = lax.axis_index("by") == lax.axis_size("by") - 1
    last_rows = jnp.where(on_top, ghost_rows, full_ext[:, :, -width:, :])
    return jnp.concatenate([full_ext[:, :, :-width, :], last_rows], axis=2)


def advance(extended, wet_ext, coriolis):
    mask_east, mask_west, mask_north, mask_south, mask_center = neighbours(wet_ext)
    val_east, val_west, val_north, val_south, val_center = neighbours(extended)
    laplace = (
        mask_east * (val_east - val_center)
        + mask_west * (val_west - val_center)
        + mask_north * (val_north - val_center)
        + mask_south * (val_south - val_center)
    )
    bound_east = mask_east * val_east + (1.0 - mask_east) * val_center
    bound_west = mask_west * val_west + (1.0 - mask_west) * val_center
    bound_north = mask_north * val_north + (1.0 - mask_north) * val_center
    bound_south = mask_south * val_south + (1.0 - mask_south) * val_center
    zonal_vel = val_center[2]
    merid_vel = val_center[3]
    advection = 0.5 * zonal_vel * (bound_east - bound_west) + 0.5 * merid_vel * (
        bound_north - bound_south
    )
    density = 0.5 * (0.8 * extended[1] - extended[0]) * wet_ext
    pressure = jnp.cumsum(density, axis=0)
    pres_east, pres_west, pres_north, pres_south, pres_center = neighbours(pressure)
    grad_x = 0.5 * (
        mask_east * pres_east
        + (1.0 - mask_east) * pres_center
        - (mask_west * pres_west + (1.0 - mask_west) * pres_center)
    )
    grad_y = 0.5 * (
        mask_north * pres_north
        + (1.0 - mask_north) * pres_center
        - (mask_south * pres_south + (1.0 - mask_south) * pres_center)
    )
    planetary = coriolis[None, :, None]
    force_zonal = planetary * merid_vel - grad_x
    force_merid = -planetary * zonal_vel - grad_y
    nothing = jnp.zeros_like(force_zonal)
    forcing = jnp.stack([nothing, nothing, force_zonal, force_merid], axis=0)
    diffusion = jnp.stack(
        [KAPPA * laplace[0], KAPPA * laplace[1], VISC * laplace[2], VISC * laplace[3]], axis=0
    )
    tendency = diffusion - advection + forcing
    return (val_center + DT * tendency) * mask_center


def local(state, level_count, coriolis):
    levels_axis = jnp.arange(state.shape[1], dtype=jnp.int32)[:, None, None]
    wet_mask = (levels_axis < level_count[None]).astype(jnp.float32)
    sign_five = jnp.array([1.0, 1.0, -1.0, -1.0, 1.0], dtype=jnp.float32)[:, None, None, None]
    sign_four = sign_five[:4]
    stacked = jnp.concatenate([state, wet_mask[None]], axis=0)
    extended = extend(stacked, sign_five, 1)
    wet_ext = extended[4]
    updated = advance(extended[:4], wet_ext, coriolis)
    updated = advance(extend(updated, sign_four, 1), wet_ext, coriolis)
    return updated


def solution(mesh):
    in_specs = (P(None, None, "by", "bx"), P("by", "bx"), P("by"))
    out_specs = P(None, None, "by", "bx")
    return jax.shard_map(local, mesh=mesh, in_specs=in_specs, out_specs=out_specs, check_vma=False)
```

profile of v0, /device:TPU:1, one launch (start us, length us, event | category | flops | bytes accessed | tf_op | source)
XLA Modules:
  0.0 151.8 jit_solution(1526689136417661426)
XLA Ops:
  0.0 0.7 fusion.42
  0.7 1.4 fusion
  2.2 0.3 copy.110
  2.5 12.9 %collective-permute-start.1 = (f32[5,8,32,1]{2,1,3,0:T(8,128)S(1)}, f32[5,8,32,1]{2,1,3,0:T(8,128)S(1)}, u32[]{:S(2)}, u32[]{:S(2)}) collective-permute-start(f32[5,8,32,1]{2,1,3,0:T(8,128)S(1)} %copy.110), channel_id=1, source_target_pairs={{16,0},{32,16},{48,32},{64,48},{80,64},{96,80},{112,96},{128,112},... | collective-permute-start | bytes 15368 | tf_op jit(solution)/shard_map/ppermute | solution.py:19
  15.4 0.3 copy.109
  15.7 1.9 %collective-permute-start = (f32[5,8,32,1]{2,1,3,0:T(8,128)S(1)}, f32[5,8,32,1]{2,1,3,0:T(8,128)S(1)}, u32[]{:S(2)}, u32[]{:S(2)}) collective-permute-start(f32[5,8,32,1]{2,1,3,0:T(8,128)S(1)} %copy.109), channel_id=1, source_target_pairs={{0,16},{16,32},{32,48},{48,64},{64,80},{80,96},{96,112},{112,128},... | collective-permute-start | bytes 15368 | tf_op jit(solution)/shard_map/ppermute | solution.py:18
  17.7 0.4 copy.91
  18.1 0.3 copy.92
  18.4 3.9 %collective-permute-done = f32[5,8,32,1]{2,1,3,0:T(8,128)S(1)} collective-permute-done((f32[5,8,32,1]{2,1,3,0:T(8,128)S(1)}, f32[5,8,32,1]{2,1,3,0:T(8,128)S(1)}, u32[]{:S(2)}, u32[]{:S(2)}) %collective-permute-start) | collective-permute-done | bytes 5152 | tf_op jit(solution)/shard_map/ppermute | solution.py:18
  22.3 0.3 copy.90
  22.7 0.1 pad_maximum_fusion.27
  22.8 1.9 %collective-permute-start.3 = (f32[5,8,1,130]{3,1,2,0:T(8,128)S(1)}, f32[5,8,1,130]{3,1,2,0:T(8,128)S(1)}, u32[]{:S(2)}, u32[]{:S(2)}) collective-permute-start(f32[5,8,1,130]{3,1,2,0:T(8,128)S(1)} %get-tuple-element.7), channel_id=1, source_target_pairs={{0,16},{16,0},{32,48},{48,32},{64,80},{80,64},{96,112},{112,96},{1... | collective-permute-start | bytes 62408 | tf_op jit(solution)/shard_map/ppermute | solution.py:25
  24.7 2.8 %collective-permute-done.3 = f32[5,8,1,130]{3,1,2,0:T(8,128)S(1)} collective-permute-done((f32[5,8,1,130]{3,1,2,0:T(8,128)S(1)}, f32[5,8,1,130]{3,1,2,0:T(8,128)S(1)}, u32[]{:S(2)}, u32[]{:S(2)}) %collective-permute-start.3) | collective-permute-done | bytes 20832 | tf_op jit(solution)/shard_map/ppermute | solution.py:25
  27.5 1.9 %collective-permute-start.4 = (f32[5,8,1,130]{3,1,2,0:T(8,128)S(1)}, f32[5,8,1,130]{3,1,2,0:T(8,128)S(1)}, u32[]{:S(2)}, u32[]{:S(2)}) collective-permute-start(f32[5,8,1,130]{3,1,2,0:T(8,128)S(1)} %collective-permute-done.3), channel_id=1, source_target_pairs={{0,32},{16,48},{32,0},{48,16},{64,96},{80,112},{96,64},{112,80},{1... | collective-permute-start | bytes 62408 | tf_op jit(solution)/shard_map/ppermute | solution.py:25
  29.4 2.8 %collective-permute-done.4 = f32[5,8,1,130]{3,1,2,0:T(8,128)S(1)} collective-permute-done((f32[5,8,1,130]{3,1,2,0:T(8,128)S(1)}, f32[5,8,1,130]{3,1,2,0:T(8,128)S(1)}, u32[]{:S(2)}, u32[]{:S(2)}) %collective-permute-start.4) | collective-permute-done | bytes 20832 | tf_op jit(solution)/shard_map/ppermute | solution.py:25
  32.2 1.9 %collective-permute-start.5 = (f32[5,8,1,130]{3,1,2,0:T(8,128)S(1)}, f32[5,8,1,130]{3,1,2,0:T(8,128)S(1)}, u32[]{:S(2)}, u32[]{:S(2)}) collective-permute-start(f32[5,8,1,130]{3,1,2,0:T(8,128)S(1)} %collective-permute-done.4), channel_id=1, source_target_pairs={{0,64},{16,80},{32,96},{48,112},{64,0},{80,16},{96,32},{112,48},{1... | collective-permute-start | bytes 62408 | tf_op jit(solution)/shard_map/ppermute | solution.py:25
  34.2 3.9 %collective-permute-done.5 = f32[5,8,1,130]{3,1,2,0:T(8,128)S(1)} collective-permute-done((f32[5,8,1,130]{3,1,2,0:T(8,128)S(1)}, f32[5,8,1,130]{3,1,2,0:T(8,128)S(1)}, u32[]{:S(2)}, u32[]{:S(2)}) %collective-permute-start.5) | collective-permute-done | bytes 20832 | tf_op jit(solution)/shard_map/ppermute | solution.py:25
  38.0 1.9 %collective-permute-start.6 = (f32[5,8,1,130]{3,1,2,0:T(8,128)S(1)}, f32[5,8,1,130]{3,1,2,0:T(8,128)S(1)}, u32[]{:S(2)}, u32[]{:S(2)}) collective-permute-start(f32[5,8,1,130]{3,1,2,0:T(8,128)S(1)} %collective-permute-done.5), channel_id=1, source_target_pairs={{0,128},{16,144},{32,160},{48,176},{64,192},{80,208},{96,224},{112... | collective-permute-start | bytes 62408 | tf_op jit(solution)/shard_map/ppermute | solution.py:25
  40.0 7.3 %collective-permute-done.6 = f32[5,8,1,130]{3,1,2,0:T(8,128)S(1)} collective-permute-done((f32[5,8,1,130]{3,1,2,0:T(8,128)S(1)}, f32[5,8,1,130]{3,1,2,0:T(8,128)S(1)}, u32[]{:S(2)}, u32[]{:S(2)}) %collective-permute-start.6) | collective-permute-done | bytes 20832 | tf_op jit(solution)/shard_map/ppermute | solution.py:25
  47.3 7.0 %collective-permute-start.7 = (f32[5,8,1,130]{3,1,2,0:T(8,128)S(1)}, f32[5,8,1,130]{3,1,2,0:T(8,128)S(1)}, u32[]{:S(2)}, u32[]{:S(2)}) collective-permute-start(f32[5,8,1,130]{3,1,2,0:T(8,128)S(1)} %collective-permute-done.6), channel_id=1, source_target_pairs={{0,256},{16,272},{32,288},{48,304},{64,320},{80,336},{96,352},{112... | collective-permute-start | bytes 62408 | tf_op jit(solution)/shard_map/ppermute | solution.py:25
  54.3 8.7 %collective-permute-start.8 = (f32[5,8,1,130]{3,1,2,0:T(8,128)S(1)}, f32[5,8,1,130]{3,1,2,0:T(8,128)S(1)}, u32[]{:S(2)}, u32[]{:S(2)}) collective-permute-start(f32[5,8,1,130]{3,1,2,0:T(8,128)S(1)} %get-tuple-element.8), channel_id=1, source_target_pairs={{1,0},{2,1},{3,2},{4,3},{5,4},{6,5},{7,6},{8,7},{9,8},{10,9},{11,1... | collective-permute-start | bytes 62408 | tf_op jit(solution)/shard_map/ppermute | solution.py:19
  63.0 0.6 copy-done.36
  63.7 0.6 pad.27.clone
  64.3 4.2 %collective-permute-start.2 = (f32[5,8,1,130]{3,1,2,0:T(8,128)S(1)}, f32[5,8,1,130]{3,1,2,0:T(8,128)S(1)}, u32[]{:S(2)}, u32[]{:S(2)}) collective-permute-start(f32[5,8,1,130]{3,1,2,0:T(8,128)S(1)} %get-tuple-element.7), channel_id=1, source_target_pairs={{0,1},{1,2},{2,3},{3,4},{4,5},{5,6},{6,7},{7,8},{8,9},{9,10},{10,1... | collective-permute-start | bytes 62408 | tf_op jit(solution)/shard_map/ppermute | solution.py:18
  68.6 0.2 reverse
  68.7 0.5 copy-done.43
  69.3 0.3 collective-permute-done.2
  69.6 1.1 fusion.17
  70.7 0.2 fusion.45
  70.9 1.5 fusion.44
  72.4 0.8 slice_multiply_fusion.15
  73.2 1.2 reduce_window_sum.17
  74.4 1.0 multiply_bitcast_fusion.3
  75.5 0.1 copy-done.7
  75.6 0.4 broadcast_subtract_fusion.3
  76.1 0.4 copy-done.2
  76.9 1.0 fusion.5
  77.9 0.2 fusion.43
  78.1 1.9 %collective-permute-start.9 = (f32[4,8,32,1]{3,1,2,0:T(8,128)S(1)}, f32[4,8,32,1]{3,1,2,0:T(8,128)S(1)}, u32[]{:S(2)}, u32[]{:S(2)}) collective-permute-start(f32[4,8,32,1]{3,1,2,0:T(8,128)S(1)} %get-tuple-element.24), channel_id=1, source_target_pairs={{16,0},{32,16},{48,32},{64,48},{80,64},{96,80},{112,96},{128,112},... | collective-permute-start | bytes 12296 | tf_op jit(solution)/shard_map/ppermute | solution.py:19
  80.0 3.4 %collective-permute-start.10 = (f32[4,8,32,1]{3,1,2,0:T(8,128)S(1)}, f32[4,8,32,1]{3,1,2,0:T(8,128)S(1)}, u32[]{:S(2)}, u32[]{:S(2)}) collective-permute-start(f32[4,8,32,1]{3,1,2,0:T(8,128)S(1)} %get-tuple-element.23), channel_id=1, source_target_pairs={{0,16},{16,32},{32,48},{48,64},{64,80},{80,96},{96,112},{112,128},... | collective-permute-start | bytes 12296 | tf_op jit(solution)/shard_map/ppermute | solution.py:18
  83.4 21.6 %collective-permute-done.9 = f32[4,8,32,1]{3,1,2,0:T(8,128)S(1)} collective-permute-done((f32[4,8,32,1]{3,1,2,0:T(8,128)S(1)}, f32[4,8,32,1]{3,1,2,0:T(8,128)S(1)}, u32[]{:S(2)}, u32[]{:S(2)}) %collective-permute-start.9) | collective-permute-done | bytes 4128 | tf_op jit(solution)/shard_map/ppermute | solution.py:19
  105.0 1.9 %collective-permute-start.11 = (f32[4,8,1,130]{3,1,2,0:T(8,128)S(1)}, f32[4,8,1,130]{3,1,2,0:T(8,128)S(1)}, u32[]{:S(2)}, u32[]{:S(2)}) collective-permute-start(f32[4,8,1,130]{3,1,2,0:T(8,128)S(1)} %get-tuple-element.9), channel_id=1, source_target_pairs={{0,16},{16,0},{32,48},{48,32},{64,80},{80,64},{96,112},{112,96},{1... | collective-permute-start | bytes 49928 | tf_op jit(solution)/shard_map/ppermute | solution.py:25
  107.0 2.7 %collective-permute-done.11 = f32[4,8,1,130]{3,1,2,0:T(8,128)S(1)} collective-permute-done((f32[4,8,1,130]{3,1,2,0:T(8,128)S(1)}, f32[4,8,1,130]{3,1,2,0:T(8,128)S(1)}, u32[]{:S(2)}, u32[]{:S(2)}) %collective-permute-start.11) | collective-permute-done | bytes 16672 | tf_op jit(solution)/shard_map/ppermute | solution.py:25
  109.7 1.9 %collective-permute-start.12 = (f32[4,8,1,130]{3,1,2,0:T(8,128)S(1)}, f32[4,8,1,130]{3,1,2,0:T(8,128)S(1)}, u32[]{:S(2)}, u32[]{:S(2)}) collective-permute-start(f32[4,8,1,130]{3,1,2,0:T(8,128)S(1)} %collective-permute-done.11), channel_id=1, source_target_pairs={{0,32},{16,48},{32,0},{48,16},{64,96},{80,112},{96,64},{112,80},{1... | collective-permute-start | bytes 49928 | tf_op jit(solution)/shard_map/ppermute | solution.py:25
  111.6 2.7 %collective-permute-done.12 = f32[4,8,1,130]{3,1,2,0:T(8,128)S(1)} collective-permute-done((f32[4,8,1,130]{3,1,2,0:T(8,128)S(1)}, f32[4,8,1,130]{3,1,2,0:T(8,128)S(1)}, u32[]{:S(2)}, u32[]{:S(2)}) %collective-permute-start.12) | collective-permute-done | bytes 16672 | tf_op jit(solution)/shard_map/ppermute | solution.py:25
  114.4 1.9 %collective-permute-start.13 = (f32[4,8,1,130]{3,1,2,0:T(8,128)S(1)}, f32[4,8,1,130]{3,1,2,0:T(8,128)S(1)}, u32[]{:S(2)}, u32[]{:S(2)}) collective-permute-start(f32[4,8,1,130]{3,1,2,0:T(8,128)S(1)} %collective-permute-done.12), channel_id=1, source_target_pairs={{0,64},{16,80},{32,96},{48,112},{64,0},{80,16},{96,32},{112,48},{1... | collective-permute-start | bytes 49928 | tf_op jit(solution)/shard_map/ppermute | solution.py:25
  116.3 3.7 %collective-permute-done.13 = f32[4,8,1,130]{3,1,2,0:T(8,128)S(1)} collective-permute-done((f32[4,8,1,130]{3,1,2,0:T(8,128)S(1)}, f32[4,8,1,130]{3,1,2,0:T(8,128)S(1)}, u32[]{:S(2)}, u32[]{:S(2)}) %collective-permute-start.13) | collective-permute-done | bytes 16672 | tf_op jit(solution)/shard_map/ppermute | solution.py:25
  120.0 3.4 %collective-permute-start.14 = (f32[4,8,1,130]{3,1,2,0:T(8,128)S(1)}, f32[4,8,1,130]{3,1,2,0:T(8,128)S(1)}, u32[]{:S(2)}, u32[]{:S(2)}) collective-permute-start(f32[4,8,1,130]{3,1,2,0:T(8,128)S(1)} %collective-permute-done.13), channel_id=1, source_target_pairs={{0,128},{16,144},{32,160},{48,176},{64,192},{80,208},{96,224},{112... | collective-permute-start | bytes 49928 | tf_op jit(solution)/shard_map/ppermute | solution.py:25
  123.3 4.8 %collective-permute-start.16 = (f32[4,8,1,130]{3,1,2,0:T(8,128)S(1)}, f32[4,8,1,130]{3,1,2,0:T(8,128)S(1)}, u32[]{:S(2)}, u32[]{:S(2)}) collective-permute-start(f32[4,8,1,130]{3,1,2,0:T(8,128)S(1)} %get-tuple-element.10), channel_id=1, source_target_pairs={{1,0},{2,1},{3,2},{4,3},{5,4},{6,5},{7,6},{8,7},{9,8},{10,9},{11,1... | collective-permute-start | bytes 49928 | tf_op jit(solution)/shard_map/ppermute | solution.py:19
  128.2 0.8 collective-permute-done.14
  129.0 6.6 %collective-permute-start.15 = (f32[4,8,1,130]{3,1,2,0:T(8,128)S(1)}, f32[4,8,1,130]{3,1,2,0:T(8,128)S(1)}, u32[]{:S(2)}, u32[]{:S(2)}) collective-permute-start(f32[4,8,1,130]{3,1,2,0:T(8,128)S(1)} %collective-permute-done.14), channel_id=1, source_target_pairs={{0,256},{16,272},{32,288},{48,304},{64,320},{80,336},{96,352},{112... | collective-permute-start | bytes 49928 | tf_op jit(solution)/shard_map/ppermute | solution.py:25
  135.6 0.7 multiply_bitcast_fusion.1
  136.4 8.8 %collective-permute-start.17 = (f32[4,8,1,130]{3,1,2,0:T(8,128)S(1)}, f32[4,8,1,130]{3,1,2,0:T(8,128)S(1)}, u32[]{:S(2)}, u32[]{:S(2)}) collective-permute-start(f32[4,8,1,130]{3,1,2,0:T(8,128)S(1)} %get-tuple-element.9), channel_id=1, source_target_pairs={{0,1},{1,2},{2,3},{3,4},{4,5},{5,6},{6,7},{7,8},{8,9},{9,10},{10,1... | collective-permute-start | bytes 49928 | tf_op jit(solution)/shard_map/ppermute | solution.py:18
  145.2 0.2 reverse.1
  145.5 0.7 collective-permute-done.17
  146.2 0.7 multiply_add_fusion
  147.0 0.8 slice_multiply_fusion.7
  147.8 0.3 fusion.13
  148.1 0.2 reduce_window_sum.18
  148.3 0.4 copy-done.37
  148.8 0.4 fusion.28
  149.2 0.4 copy-done.9
  150.1 0.8 fusion.9
  150.9 0.9 copy.108
  (94 shorter events, 1.4 us)
Async XLA Ops:
  2.2 15.4 %copy-start = (f32[4,8,32,128]{3,2,1,0:T(8,128)S(1)}, f32[4,8,32,128]{3,2,1,0:T(8,128)}, u32[]{:S(2)}) copy-start(f32[4,8,32,128]{3,2,1,0:T(8,128)} %param.4) | copy-start | bytes 1572868
  2.5 15.6 %collective-permute-start.1 = (f32[5,8,32,1]{2,1,3,0:T(8,128)S(1)}, f32[5,8,32,1]{2,1,3,0:T(8,128)S(1)}, u32[]{:S(2)}, u32[]{:S(2)}) collective-permute-start(f32[5,8,32,1]{2,1,3,0:T(8,128)S(1)} %copy.110), channel_id=1, source_target_pairs={{16,0},{32,16},{48,32},{64,48},{80,64},{96,80},{112,96},{128,112},... | collective-permute-start | bytes 15368 | tf_op jit(solution)/shard_map/ppermute | solution.py:19
  15.7 6.6 %collective-permute-start = (f32[5,8,32,1]{2,1,3,0:T(8,128)S(1)}, f32[5,8,32,1]{2,1,3,0:T(8,128)S(1)}, u32[]{:S(2)}, u32[]{:S(2)}) collective-permute-start(f32[5,8,32,1]{2,1,3,0:T(8,128)S(1)} %copy.109), channel_id=1, source_target_pairs={{0,16},{16,32},{32,48},{48,64},{64,80},{80,96},{96,112},{112,128},... | collective-permute-start | bytes 15368 | tf_op jit(solution)/shard_map/ppermute | solution.py:18
  22.8 4.7 %collective-permute-start.3 = (f32[5,8,1,130]{3,1,2,0:T(8,128)S(1)}, f32[5,8,1,130]{3,1,2,0:T(8,128)S(1)}, u32[]{:S(2)}, u32[]{:S(2)}) collective-permute-start(f32[5,8,1,130]{3,1,2,0:T(8,128)S(1)} %get-tuple-element.7), channel_id=1, source_target_pairs={{0,16},{16,0},{32,48},{48,32},{64,80},{80,64},{96,112},{112,96},{1... | collective-permute-start | bytes 62408 | tf_op jit(solution)/shard_map/ppermute | solution.py:25
  27.5 4.7 %collective-permute-start.4 = (f32[5,8,1,130]{3,1,2,0:T(8,128)S(1)}, f32[5,8,1,130]{3,1,2,0:T(8,128)S(1)}, u32[]{:S(2)}, u32[]{:S(2)}) collective-permute-start(f32[5,8,1,130]{3,1,2,0:T(8,128)S(1)} %collective-permute-done.3), channel_id=1, source_target_pairs={{0,32},{16,48},{32,0},{48,16},{64,96},{80,112},{96,64},{112,80},{1... | collective-permute-start | bytes 62408 | tf_op jit(solution)/shard_map/ppermute | solution.py:25
  32.2 5.8 %collective-permute-start.5 = (f32[5,8,1,130]{3,1,2,0:T(8,128)S(1)}, f32[5,8,1,130]{3,1,2,0:T(8,128)S(1)}, u32[]{:S(2)}, u32[]{:S(2)}) collective-permute-start(f32[5,8,1,130]{3,1,2,0:T(8,128)S(1)} %collective-permute-done.4), channel_id=1, source_target_pairs={{0,64},{16,80},{32,96},{48,112},{64,0},{80,16},{96,32},{112,48},{1... | collective-permute-start | bytes 62408 | tf_op jit(solution)/shard_map/ppermute | solution.py:25
  38.0 9.2 %collective-permute-start.6 = (f32[5,8,1,130]{3,1,2,0:T(8,128)S(1)}, f32[5,8,1,130]{3,1,2,0:T(8,128)S(1)}, u32[]{:S(2)}, u32[]{:S(2)}) collective-permute-start(f32[5,8,1,130]{3,1,2,0:T(8,128)S(1)} %collective-permute-done.5), channel_id=1, source_target_pairs={{0,128},{16,144},{32,160},{48,176},{64,192},{80,208},{96,224},{112... | collective-permute-start | bytes 62408 | tf_op jit(solution)/shard_map/ppermute | solution.py:25
  47.3 21.2 %collective-permute-start.7 = (f32[5,8,1,130]{3,1,2,0:T(8,128)S(1)}, f32[5,8,1,130]{3,1,2,0:T(8,128)S(1)}, u32[]{:S(2)}, u32[]{:S(2)}) collective-permute-start(f32[5,8,1,130]{3,1,2,0:T(8,128)S(1)} %collective-permute-done.6), channel_id=1, source_target_pairs={{0,256},{16,272},{32,288},{48,304},{64,320},{80,336},{96,352},{112... | collective-permute-start | bytes 62408 | tf_op jit(solution)/shard_map/ppermute | solution.py:25
  54.3 14.4 %collective-permute-start.8 = (f32[5,8,1,130]{3,1,2,0:T(8,128)S(1)}, f32[5,8,1,130]{3,1,2,0:T(8,128)S(1)}, u32[]{:S(2)}, u32[]{:S(2)}) collective-permute-start(f32[5,8,1,130]{3,1,2,0:T(8,128)S(1)} %get-tuple-element.8), channel_id=1, source_target_pairs={{1,0},{2,1},{3,2},{4,3},{5,4},{6,5},{7,6},{8,7},{9,8},{10,9},{11,1... | collective-permute-start | bytes 62408 | tf_op jit(solution)/shard_map/ppermute | solution.py:19
  63.0 0.7 copy-start.36
  63.7 11.8 %copy-start.40 = (f32[32]{0:T(128)}, f32[32]{0:T(128)S(1)}, u32[]{:S(2)}) copy-start(f32[32]{0:T(128)S(1)} %neg.5) | copy-start | bytes 388
  64.3 5.3 %collective-permute-start.2 = (f32[5,8,1,130]{3,1,2,0:T(8,128)S(1)}, f32[5,8,1,130]{3,1,2,0:T(8,128)S(1)}, u32[]{:S(2)}, u32[]{:S(2)}) collective-permute-start(f32[5,8,1,130]{3,1,2,0:T(8,128)S(1)} %get-tuple-element.7), channel_id=1, source_target_pairs={{0,1},{1,2},{2,3},{3,4},{4,5},{5,6},{6,7},{7,8},{8,9},{9,10},{10,1... | collective-permute-start | bytes 62408 | tf_op jit(solution)/shard_map/ppermute | solution.py:18
  68.5 0.7 copy-start.43
  69.3 1.6 %copy-start.18 = (f32[5,8,1,130]{3,1,2,0:T(8,128)}, f32[5,8,1,130]{3,1,2,0:T(8,128)S(1)}, u32[]{:S(2)}) copy-start(f32[5,8,1,130]{3,1,2,0:T(8,128)S(1)} %multiply_select_fusion) | copy-start | bytes 62404
  69.6 1.3 copy-start.32
  70.9 1.5 %copy-start.1 = (f32[8,32,128]{2,0,1:T(8,128)}, f32[8,32,128]{2,0,1:T(8,128)S(1)}, u32[]{:S(2)}) copy-start(f32[8,32,128]{2,0,1:T(8,128)S(1)} %get-tuple-element.42) | copy-start | bytes 393220
  70.9 1.5 copy-start.4
  74.4 1.2 copy-start.7
  75.6 0.9 copy-start.2
  75.6 1.0 copy-start.5
  75.6 1.0 copy-start.19
  75.6 1.0 copy-start.28
  75.6 1.1 copy-start.29
  75.6 1.2 copy-start.30
  75.6 1.2 copy-start.31
  75.6 1.2 copy-start.33
  76.1 1.8 %copy-start.8 = (f32[8,32,128]{2,0,1:T(8,128)}, f32[8,32,128]{2,0,1:T(8,128)S(1)}, u32[]{:S(2)}) copy-start(f32[8,32,128]{2,0,1:T(8,128)S(1)} %get-tuple-element.33) | copy-start | bytes 393220
  76.1 1.8 %copy-start.10 = (f32[8,32,128]{2,0,1:T(8,128)}, f32[8,32,128]{2,0,1:T(8,128)S(1)}, u32[]{:S(2)}) copy-start(f32[8,32,128]{2,0,1:T(8,128)S(1)} %get-tuple-element.34) | copy-start | bytes 393220
  76.1 1.8 %copy-start.12 = (f32[8,32,128]{2,0,1:T(8,128)}, f32[8,32,128]{2,0,1:T(8,128)S(1)}, u32[]{:S(2)}) copy-start(f32[8,32,128]{2,0,1:T(8,128)S(1)} %get-tuple-element.37) | copy-start | bytes 393220
  76.1 1.8 %copy-start.14 = (f32[8,32,128]{2,0,1:T(8,128)}, f32[8,32,128]{2,0,1:T(8,128)S(1)}, u32[]{:S(2)}) copy-start(f32[8,32,128]{2,0,1:T(8,128)S(1)} %get-tuple-element.38) | copy-start | bytes 393220
  76.1 1.8 %copy-start.16 = (f32[8,32,128]{2,0,1:T(8,128)}, f32[8,32,128]{2,0,1:T(8,128)S(1)}, u32[]{:S(2)}) copy-start(f32[8,32,128]{2,0,1:T(8,128)S(1)} %get-tuple-element.39) | copy-start | bytes 393220
  76.1 0.8 copy-start.38
  78.1 26.9 %collective-permute-start.9 = (f32[4,8,32,1]{3,1,2,0:T(8,128)S(1)}, f32[4,8,32,1]{3,1,2,0:T(8,128)S(1)}, u32[]{:S(2)}, u32[]{:S(2)}) collective-permute-start(f32[4,8,32,1]{3,1,2,0:T(8,128)S(1)} %get-tuple-element.24), channel_id=1, source_target_pairs={{16,0},{32,16},{48,32},{64,48},{80,64},{96,80},{112,96},{128,112},... | collective-permute-start | bytes 12296 | tf_op jit(solution)/shard_map/ppermute | solution.py:19
  80.0 24.9 %collective-permute-start.10 = (f32[4,8,32,1]{3,1,2,0:T(8,128)S(1)}, f32[4,8,32,1]{3,1,2,0:T(8,128)S(1)}, u32[]{:S(2)}, u32[]{:S(2)}) collective-permute-start(f32[4,8,32,1]{3,1,2,0:T(8,128)S(1)} %get-tuple-element.23), channel_id=1, source_target_pairs={{0,16},{16,32},{32,48},{48,64},{64,80},{80,96},{96,112},{112,128},... | collective-permute-start | bytes 12296 | tf_op jit(solution)/shard_map/ppermute | solution.py:18
  105.0 4.7 %collective-permute-start.11 = (f32[4,8,1,130]{3,1,2,0:T(8,128)S(1)}, f32[4,8,1,130]{3,1,2,0:T(8,128)S(1)}, u32[]{:S(2)}, u32[]{:S(2)}) collective-permute-start(f32[4,8,1,130]{3,1,2,0:T(8,128)S(1)} %get-tuple-element.9), channel_id=1, source_target_pairs={{0,16},{16,0},{32,48},{48,32},{64,80},{80,64},{96,112},{112,96},{1... | collective-permute-start | bytes 49928 | tf_op jit(solution)/shard_map/ppermute | solution.py:25
  109.7 4.6 %collective-permute-start.12 = (f32[4,8,1,130]{3,1,2,0:T(8,128)S(1)}, f32[4,8,1,130]{3,1,2,0:T(8,128)S(1)}, u32[]{:S(2)}, u32[]{:S(2)}) collective-permute-start(f32[4,8,1,130]{3,1,2,0:T(8,128)S(1)} %collective-permute-done.11), channel_id=1, source_target_pairs={{0,32},{16,48},{32,0},{48,16},{64,96},{80,112},{96,64},{112,80},{1... | collective-permute-start | bytes 49928 | tf_op jit(solution)/shard_map/ppermute | solution.py:25
  114.4 5.6 %collective-permute-start.13 = (f32[4,8,1,130]{3,1,2,0:T(8,128)S(1)}, f32[4,8,1,130]{3,1,2,0:T(8,128)S(1)}, u32[]{:S(2)}, u32[]{:S(2)}) collective-permute-start(f32[4,8,1,130]{3,1,2,0:T(8,128)S(1)} %collective-permute-done.12), channel_id=1, source_target_pairs={{0,64},{16,80},{32,96},{48,112},{64,0},{80,16},{96,32},{112,48},{1... | collective-permute-start | bytes 49928 | tf_op jit(solution)/shard_map/ppermute | solution.py:25
  120.0 9.0 %collective-permute-start.14 = (f32[4,8,1,130]{3,1,2,0:T(8,128)S(1)}, f32[4,8,1,130]{3,1,2,0:T(8,128)S(1)}, u32[]{:S(2)}, u32[]{:S(2)}) collective-permute-start(f32[4,8,1,130]{3,1,2,0:T(8,128)S(1)} %collective-permute-done.13), channel_id=1, source_target_pairs={{0,128},{16,144},{32,160},{48,176},{64,192},{80,208},{96,224},{112... | collective-permute-start | bytes 49928 | tf_op jit(solution)/shard_map/ppermute | solution.py:25
  123.3 22.0 %collective-permute-start.16 = (f32[4,8,1,130]{3,1,2,0:T(8,128)S(1)}, f32[4,8,1,130]{3,1,2,0:T(8,128)S(1)}, u32[]{:S(2)}, u32[]{:S(2)}) collective-permute-start(f32[4,8,1,130]{3,1,2,0:T(8,128)S(1)} %get-tuple-element.10), channel_id=1, source_target_pairs={{1,0},{2,1},{3,2},{4,3},{5,4},{6,5},{7,6},{8,7},{9,8},{10,9},{11,1... | collective-permute-start | bytes 49928 | tf_op jit(solution)/shard_map/ppermute | solution.py:19
  129.0 16.2 %collective-permute-start.15 = (f32[4,8,1,130]{3,1,2,0:T(8,128)S(1)}, f32[4,8,1,130]{3,1,2,0:T(8,128)S(1)}, u32[]{:S(2)}, u32[]{:S(2)}) collective-permute-start(f32[4,8,1,130]{3,1,2,0:T(8,128)S(1)} %collective-permute-done.14), channel_id=1, source_target_pairs={{0,256},{16,272},{32,288},{48,304},{64,320},{80,336},{96,352},{112... | collective-permute-start | bytes 49928 | tf_op jit(solution)/shard_map/ppermute | solution.py:25
  135.6 9.8 %copy-start.42 = (f32[4]{0:T(128)S(1)}, f32[4]{0:T(128)}, u32[]{:S(2)}) copy-start(f32[4]{0:T(128)} %constant.26) | copy-start | bytes 52
  135.6 10.6 %copy-start.6 = (f32[8,32,128]{2,0,1:T(8,128)S(1)}, f32[8,32,128]{2,0,1:T(8,128)}, u32[]{:S(2)}) copy-start(f32[8,32,128]{2,0,1:T(8,128)} %copy-done.4) | copy-start | bytes 393220
  136.4 9.8 %copy-start.3 = (f32[8,32,128]{2,0,1:T(8,128)S(1)}, f32[8,32,128]{2,0,1:T(8,128)}, u32[]{:S(2)}) copy-start(f32[8,32,128]{2,0,1:T(8,128)} %copy-done.1) | copy-start | bytes 393220
  136.4 9.8 %collective-permute-start.17 = (f32[4,8,1,130]{3,1,2,0:T(8,128)S(1)}, f32[4,8,1,130]{3,1,2,0:T(8,128)S(1)}, u32[]{:S(2)}, u32[]{:S(2)}) collective-permute-start(f32[4,8,1,130]{3,1,2,0:T(8,128)S(1)} %get-tuple-element.9), channel_id=1, source_target_pairs={{0,1},{1,2},{2,3},{3,4},{4,5},{5,6},{6,7},{7,8},{8,9},{9,10},{10,1... | collective-permute-start | bytes 49928 | tf_op jit(solution)/shard_map/ppermute | solution.py:18
  145.5 2.3 %copy-start.20 = (f32[4,8,1,130]{3,1,2,0:T(8,128)}, f32[4,8,1,130]{3,1,2,0:T(8,128)S(1)}, u32[]{:S(2)}) copy-start(f32[4,8,1,130]{3,1,2,0:T(8,128)S(1)} %multiply_select_fusion.1) | copy-start | bytes 49924
  146.2 1.6 %copy-start.34 = (f32[4,8,1,130]{3,1,2,0:T(8,128)}, f32[4,8,1,130]{3,1,2,0:T(8,128)S(1)}, u32[]{:S(2)}) copy-start(f32[4,8,1,130]{3,1,2,0:T(8,128)S(1)} %collective-permute-done.17) | copy-start | bytes 49924
  148.0 0.7 copy-start.37
  148.1 0.6 copy-start.41
  148.7 0.9 copy-start.9
  148.7 1.0 copy-start.11
  148.7 1.0 copy-start.13
  148.7 1.1 copy-start.15
  148.7 1.1 copy-start.17
  148.7 1.1 copy-start.21
  148.7 1.2 copy-start.22
  148.8 1.2 copy-start.23
  148.8 1.2 copy-start.24
  148.8 1.3 copy-start.25
  148.8 1.3 copy-start.26
  148.8 1.3 copy-start.27
  148.8 1.3 copy-start.35
  149.2 0.9 copy-start.39
where the time goes:
time: 154 us; the launch traced here: 152 us
  starting transfers between devices  77.1 us (50%)
  waiting for transfers between devices  53.3 us (35%)
  other arithmetic  13.5 us (9%)
  local copies, waits for them, and re-layouts  7.24 us (5%)
    ppermute x10, starting transfers between devices, swapped(): lax.ppermute(value, axis, [(i, i ^ 1 << apart) for i in range(lax.axis_si...  30.4 us
    ppermute x4, starting transfers between devices, padded(): after = lax.ppermute(initial, axis, down)  28.3 us
    ppermute x10, waiting for transfers between devices, swapped(): lax.ppermute(value, axis, [(i, i ^ 1 << apart) for i in range(lax.axis_si...  26.8 us
    ppermute x4, waiting for transfers between devices, padded(): after = lax.ppermute(initial, axis, down)  21.6 us
    ppermute x4, starting transfers between devices, padded(): before = lax.ppermute(last, axis, up)  18.3 us
    ppermute x4, waiting for transfers between devices, padded(): before = lax.ppermute(last, axis, up)  4.94 us
    unnamed x92, local copies, waits for them, and re-layouts  4.36 us
  transfers between devices with their start and end apart: 18, of which 12 were waited for; matrix products, arithmetic and copies ran while one was open for 2% of the time, Pallas kernels for 0%

commit v1 on v0

v1 whole, which is shorter than its diff:
```python
import functools

import jax
import jax.numpy as jnp
from jax import lax
from jax.experimental import pallas as pl
from jax.experimental.pallas import tpu as pltpu
from jax.sharding import PartitionSpec as P

MESH = pl.DeviceIdType.MESH
FIELDS, LEV, CY, CX = 4, 8, 32, 128
DT = 0.2
COEF = (DT * 0.5, DT * 0.5, DT * 0.4, DT * 0.4)
HALF = DT * 0.5
WEST, EAST = 0, 1
SOUTH, NORTH = 0, 1
SW, NW, SE, NE = 0, 1, 2, 3


def update(center, ahead, behind, inner, outer, pressures, masks, along, sign_across, planetary):
    across = 5 - along
    m_c, m_a, m_b, m_i, m_o = masks
    p_c, p_a, p_b, p_i, p_o = pressures
    h_along = HALF * center[along]
    h_across = sign_across * (HALF * center[across])
    grad_along = HALF * (jnp.where(m_a, p_a, p_c) - jnp.where(m_b, p_b, p_c))
    grad_across = sign_across * (HALF * (jnp.where(m_i, p_i, p_c) - jnp.where(m_o, p_o, p_c)))
    grad = {along: grad_along, across: grad_across}
    turn = DT * planetary
    force = {2: turn * center[3] - grad[2], 3: -turn * center[2] - grad[3]}
    result = []
    for f in range(FIELDS):
        c = center[f]
        b_a, b_b = jnp.where(m_a, ahead[f], c), jnp.where(m_b, behind[f], c)
        b_i, b_o = jnp.where(m_i, inner[f], c), jnp.where(m_o, outer[f], c)
        new = (1.0 - 4.0 * COEF[f]) * c + COEF[f] * ((b_a + b_b) + (b_i + b_o))
        new = new - h_along * (b_a - b_b) - h_across * (b_i - b_o)
        if f >= 2:
            new = new + force[f]
        result.append(jnp.where(m_c, new, 0.0))
    return result


def strip_step(lines, depths, turns, wanted, along, sign_across):
    level = lax.broadcasted_iota(jnp.int32, (LEV, CX), 0)
    level_f = level.astype(jnp.float32)

    def pressure_of(j):
        total = jnp.where(level_f < depths[j], 0.4 * lines[j][1] - 0.5 * lines[j][0], 0.0)
        for shift in (1, 2, 4):
            total = total + jnp.where(level >= shift, pltpu.roll(total, shift, 0), 0.0)
        return total

    pressures = {j: pressure_of(j) for j in range(min(wanted) - 1, max(wanted) + 2)}

    def ahead(x):
        return pltpu.roll(x, CX - 1, 1)

    def behind(x):
        return pltpu.roll(x, 1, 1)

    result = {}
    for j in wanted:
        center, p = lines[j], pressures[j]
        masks = [
            level_f < d
            for d in (depths[j], ahead(depths[j]), behind(depths[j]), depths[j + 1], depths[j - 1])
        ]
        result[j] = update(
            center,
            [ahead(x) for x in center],
            [behind(x) for x in center],
            lines[j + 1],
            lines[j - 1],
            (p, ahead(p), behind(p), pressures[j + 1], pressures[j - 1]),
            masks,
            along,
            sign_across,
            turns[j],
        )
    return result


def block_step(src, dst, depth, planetary):
    d_e, d_w = pltpu.roll(depth, CX - 1, 1), pltpu.roll(depth, 1, 1)
    d_n, d_s = pltpu.roll(depth, CY - 1, 0), pltpu.roll(depth, 1, 0)

    def level_step(k, p):
        kf = k.astype(jnp.float32)
        center = [src[pl.ds(pl.multiple_of(f * LEV * CY + k * CY, CY), CY), :] for f in range(FIELDS)]
        masks = [kf < d for d in (depth, d_e, d_w, d_n, d_s)]
        p = p + jnp.where(masks[0], 0.4 * center[1] - 0.5 * center[0], 0.0)

        def moved(x):
            return (pltpu.roll(x, CX - 1, 1), pltpu.roll(x, 1, 1), pltpu.roll(x, CY - 1, 0), pltpu.roll(x, 1, 0))

        around = [moved(x) for x in center]
        new = update(
            center, *[[a[i] for a in around] for i in range(4)], (p, *moved(p)), masks, 2, 1.0, planetary
        )
        for f in range(FIELDS):
            dst[pl.ds(pl.multiple_of(f * LEV * CY + k * CY, CY), CY), :] = new[f]
        return p

    lax.fori_loop(0, LEV, level_step, jnp.zeros((CY, CX), jnp.float32))


def kernel(
    nb, ny, state, level_count, coriolis, out,
    x, y, depth_i, depth, turn_s, turn, tall, packed, ew_out, ns_out, co_out, ew_in, ns_in, co_in,
    load_sem, send_sem, recv_sem,
):
    bx, by = lax.axis_index("bx"), lax.axis_index("by")
    top = by // (ny - 1)
    east, west = lax.rem(bx + 1, nb), lax.rem(bx + nb - 1, nb)

    def north(column):
        return column + top * (nb - 1 - 2 * column), by + 1 - top

    has_south = by > 0
    south = by - 1
    flip = 1.0 - 2.0 * top.astype(jnp.float32)

    ne_to, nw_to = north(east), north(west)
    ne_other = jnp.logical_or(ne_to[0] != bx, ne_to[1] != by)
    nw_other = jnp.logical_or(nw_to[0] != bx, nw_to[1] != by)
    plan = [
        (ew_out.at[0], ew_in.at[WEST], WEST, (east, by), None),
        (ew_out.at[1], ew_in.at[EAST], EAST, (west, by), None),
        (co_out.at[0], co_in.at[SW + (NE - SW) * top], 4 + SW + (NE - SW) * top, ne_to, ne_other),
        (co_out.at[1], co_in.at[SE + (NW - SE) * top], 4 + SE + (NW - SE) * top, nw_to, nw_other),
        (co_out.at[2], co_in.at[NW], 4 + NW, (east, south), has_south),
        (co_out.at[3], co_in.at[NE], 4 + NE, (west, south), has_south),
        (ns_out.at[0], ns_in.at[SOUTH + top], 2 + SOUTH + top, north(bx), None),
        (ns_out.at[1], ns_in.at[NORTH], 2 + NORTH, (bx, south), has_south),
    ]

    def when(condition, run):
        if condition is None:
            run()
        else:
            pl.when(condition)(run)

    barrier = pltpu.get_barrier_semaphore()
    partners = jnp.int32(0)
    for _, _, _, device, condition in plan:
        when(condition, functools.partial(
            pl.semaphore_signal, barrier, inc=1, device_id=device, device_id_type=MESH))
        partners = partners + (1 if condition is None else condition.astype(jnp.int32))

    loads = [
        pltpu.make_async_copy(level_count, depth_i, load_sem.at[FIELDS]),
        pltpu.make_async_copy(coriolis, turn_s, load_sem.at[FIELDS + 1]),
    ] + [
        pltpu.make_async_copy(
            state.at[pl.ds(f * LEV * CY, LEV * CY)], x.at[pl.ds(f * LEV * CY, LEV * CY)], load_sem.at[f])
        for f in range(FIELDS)
    ]
    for load in loads:
        load.start()

    lane = lax.broadcasted_iota(jnp.int32, (LEV, CX), 1)
    level = lax.broadcasted_iota(jnp.int32, (LEV, CX), 0)
    lane_tall = lax.broadcasted_iota(jnp.int32, (CY, CX), 1)
    left = lane < 64

    @pl.when(jnp.logical_not(has_south))
    def _():
        ns_in[SOUTH] = jnp.zeros((9, LEV, CX), jnp.float32)
        co_in[SW] = jnp.zeros((LEV, CX), jnp.float32)
        co_in[SE] = jnp.zeros((LEV, CX), jnp.float32)

    def transposed(group, value):
        tall[group, pl.ds(2, CY), :] = value
        tall[group, pl.ds(66, CY), :] = value
        packed[group] = tall[group].T

    for load in loads[:2]:
        load.wait()
    depth[...] = depth_i[...].astype(jnp.float32)
    for r in range(CY):
        turn[pl.ds(r, 1), :] = jnp.full((1, CX), turn_s[r], jnp.float32)
    transposed(2, pltpu.roll(depth[...], 4, 1))

    for group in range(2):
        value = jnp.zeros((CY, CX), jnp.float32)
        for q in range(16):
            if q % LEV == 0:
                loads[2 + 2 * group + q // LEV].wait()
            moved = pltpu.roll(x[pl.ds((16 * group + q) * CY, CY), :], (8 * q + 4) % CX, 1)
            value = jnp.where(lane_tall // 8 == q, moved, value)
        transposed(group, value)

    def column(f, c):
        if f == FIELDS:
            return jnp.broadcast_to(packed[2, pl.ds(c, 1), :], (LEV, CX))
        return packed[f // 2, pl.ds((f % 2) * 64 + c, LEV, stride=8), :]

    def row(ref, f, r):
        return ref[pl.ds(f * LEV * CY + r, LEV, stride=CY), :]

    corners = [jnp.zeros((LEV, CX), jnp.float32) for _ in range(4)]
    for f in range(FIELDS + 1):
        edge_w, edge_e = column(f, 4), column(f, 3)
        ew_out[0, f] = jnp.where(left, edge_e, column(f, 2))
        ew_out[1, f] = jnp.where(left, column(f, 5), edge_w)
        s = 4 * f
        if f in (2, 3):
            fold_e, fold_w = edge_e * flip, edge_w * flip
        else:
            fold_e, fold_w = edge_e, edge_w

        def put(i, at, value):
            corners[i] = jnp.where(lane == at + s, value, corners[i])

        put(0, 1, pltpu.roll(fold_e, (96 + s) % CX, 1))
        put(0, 98, pltpu.roll(fold_e, 1 + s, 1))
        put(1, 65, pltpu.roll(fold_w, (96 + s) % CX, 1))
        put(1, 34, pltpu.roll(fold_w, 1 + s, 1))
        put(2, 34, pltpu.roll(edge_e, 32 + s, 1))
        put(3, 98, pltpu.roll(edge_w, 32 + s, 1))
    for i in range(4):
        co_out[i] = corners[i]

    for side, rows in ((0, (31, 30)), (1, (0, 1))):
        for f in range(FIELDS):
            for i, r in enumerate(rows):
                ns_out[side, 2 * f + i] = row(x, f, r)
        ns_out[side, 8] = jnp.where(
            level == 0, depth[pl.ds(rows[0], 1), :],
            jnp.where(level == 1, depth[pl.ds(rows[1], 1), :], turn[pl.ds(rows[0], 1), :]))

    @pl.when(top == 1)
    def _():
        for i in range(9):
            mirrored = jnp.take_along_axis(ns_out[0, i], (CX - 1) - lane, axis=1)
            ns_out[0, i] = -mirrored if i in (4, 5, 6, 7) else mirrored

    pl.semaphore_wait(barrier, partners)
    sends = []
    for i, (source, target, slot, device, condition) in enumerate(plan):
        copy = pltpu.make_async_remote_copy(
            src_ref=source, dst_ref=target, send_sem=send_sem.at[i], recv_sem=recv_sem.at[slot],
            device_id=device, device_id_type=MESH)
        when(condition, copy.start)
        sends.append((copy, condition))

    @pl.when(jnp.logical_not(ne_other))
    def _():
        co_in[NE] = co_out[0]

    @pl.when(jnp.logical_not(nw_other))
    def _():
        co_in[NW] = co_out[1]

    block_step(x, y, depth[...], turn[...])
    block_step(y, out, depth[...], turn[...])

    def received(ref, slot, condition):
        copy = pltpu.make_async_remote_copy(
            src_ref=ref, dst_ref=ref, send_sem=send_sem.at[0], recv_sem=recv_sem.at[slot],
            device_id=(east, by), device_id_type=MESH)
        when(condition, copy.wait_recv)

    received(ns_in.at[SOUTH], 2 + SOUTH, has_south)
    received(ns_in.at[NORTH], 2 + NORTH, None)

    def spread(ref, r):
        return jnp.broadcast_to(ref[pl.ds(r, 1), :], (LEV, CX))

    def from_halo(side, f, i):
        if f == FIELDS:
            return jnp.broadcast_to(ns_in[side, 8, pl.ds(i, 1), :], (LEV, CX))
        return ns_in[side, 2 * f + i]

    for side, rows, sign in ((SOUTH, (0, 1, 2), 1.0), (NORTH, (31, 30, 29), -1.0)):
        lines = {-1 - i: [from_halo(side, f, i) for f in range(FIELDS)] for i in range(2)}
        lines |= {j: [row(x, f, rows[j]) for f in range(FIELDS)] for j in range(2)}
        depths = {-1 - i: from_halo(side, FIELDS, i) for i in range(2)}
        depths |= {j: spread(depth, rows[j]) for j in range(3)}
        turns = {-1: from_halo(side, FIELDS, 2)} | {j: spread(turn, rows[j]) for j in range(2)}
        first = strip_step(lines, depths, turns, (-1, 0), 2, sign)
        first |= {j: [row(y, f, rows[j]) for f in range(FIELDS)] for j in (1, 2)}
        second = strip_step(first, depths, turns, (0, 1), 2, sign)
        for j in range(2):
            for f in range(FIELDS):
                out[pl.ds(f * LEV * CY + rows[j], LEV, stride=CY), :] = second[j][f]

    def at_rows(j, f):
        value = jnp.where(left, column(f, 4 + j), column(f, 3 - j))
        if j == 3:
            return value
        for side, i, at in ((SOUTH, 0, 1), (SOUTH, 1, 0), (NORTH, 0, 34), (NORTH, 1, 35)):
            if j == 2 and i == 1:
                continue
            halo = from_halo(side, f, i)
            halo = jnp.where(left, halo[:, j : j + 1], halo[:, CX - 1 - j : CX - j])
            value = jnp.where(lane % 64 == at, halo, value)
        return value

    lines = {j: [at_rows(j, f) for f in range(FIELDS)] for j in range(4)}
    depths = {j: at_rows(j, FIELDS) for j in range(4)}
    planetary = jnp.where(lane % 64 == 1, from_halo(SOUTH, FIELDS, 2), from_halo(NORTH, FIELDS, 2))
    for r in range(CY):
        planetary = jnp.where(lane % 64 == r + 2, turn_s[r], planetary)
    turns = {j: planetary for j in range(-1, 3)}
    sign = jnp.where(left, 1.0, -1.0)
    first = strip_step(lines, depths, turns, (1, 2), 3, sign)

    received(co_in.at[SW], 4 + SW, has_south)
    received(co_in.at[SE], 4 + SE, has_south)
    received(co_in.at[NW], 4 + NW, nw_other)
    received(co_in.at[NE], 4 + NE, ne_other)
    received(ew_in.at[WEST], WEST, None)
    received(ew_in.at[EAST], EAST, None)

    corner = jnp.where(
        left, jnp.where(lane < 32, co_in[SW], co_in[NW]), jnp.where(lane < 96, co_in[SE], co_in[NE]))
    at_corner = jnp.logical_or(lane % 64 == 1, lane % 64 == 34)

    def outside(f):
        near = jnp.where(left, ew_in[WEST, f], ew_in[EAST, f])
        far = jnp.where(left, ew_in[EAST, f], ew_in[WEST, f])
        shifted = corner if f == 0 else pltpu.roll(corner, CX - 4 * f, 1)
        return jnp.where(at_corner, shifted, near), pltpu.roll(far, 64, 1)

    beyond = [outside(f) for f in range(FIELDS + 1)]
    for i in range(2):
        lines[-1 - i] = [beyond[f][i] for f in range(FIELDS)]
        depths[-1 - i] = beyond[FIELDS][i]
    first |= strip_step(lines, depths, turns, (-1, 0), 3, sign)
    second = strip_step(first, depths, turns, (0, 1), 3, sign)
    for f in range(FIELDS):
        for c, j, shift in ((0, 1, 62), (1, 0, 62), (2, 0, 126), (3, 1, 126)):
            packed[0, pl.ds(f * 32 + c, LEV, stride=4), :] = pltpu.roll(second[j][f], shift, 1)
    edges = packed[0].T[:CY]
    at_edge = jnp.logical_or(lane_tall < 2, lane_tall >= CX - 2)
    for p in range(FIELDS * LEV):
        moved = pltpu.roll(edges, (126 - 4 * p) % CX, 1)
        spot = out.at[pl.ds(p * CY, CY)]
        spot[...] = jnp.where(at_edge, moved, spot[...])

    for copy, condition in sends:
        when(condition, copy.wait_send)


def local(nb, ny, state, level_count, coriolis):
    vmem = pltpu.VMEM
    f32 = jnp.float32
    result = pl.pallas_call(
        functools.partial(kernel, nb, ny),
        out_shape=vmem((FIELDS * LEV * CY, CX), f32),
        in_specs=[pl.BlockSpec(memory_space=pltpu.HBM)] * 3,
        out_specs=pl.BlockSpec(memory_space=pltpu.VMEM),
        scratch_shapes=[
            vmem((FIELDS * LEV * CY, CX), f32),
            vmem((FIELDS * LEV * CY, CX), f32),
            vmem((CY, CX), jnp.int32),
            vmem((CY, CX), f32),
            pltpu.SMEM((CY,), f32),
            vmem((CY, CX), f32),
            vmem((3, CX, CX), f32),
            vmem((3, CX, CX), f32),
            vmem((2, 5, LEV, CX), f32),
            vmem((2, 9, LEV, CX), f32),
            vmem((4, LEV, CX), f32),
            vmem((2, 5, LEV, CX), f32),
            vmem((2, 9, LEV, CX), f32),
            vmem((4, LEV, CX), f32),
            pltpu.SemaphoreType.DMA((FIELDS + 2,)),
            pltpu.SemaphoreType.DMA((8,)),
            pltpu.SemaphoreType.DMA((8,)),
        ],
        compiler_params=pltpu.CompilerParams(collective_id=0, has_side_effects=True),
    )(state.reshape(FIELDS * LEV * CY, CX), level_count, coriolis)
    return result.reshape(FIELDS, LEV, CY, CX)


def solution(mesh):
    nb, ny = mesh.shape["bx"], mesh.shape["by"]
    in_specs = (P(None, None, "by", "bx"), P("by", "bx"), P("by"))
    out_specs = P(None, None, "by", "bx")
    return jax.shard_map(
        functools.partial(local, nb, ny), mesh=mesh, in_specs=in_specs, out_specs=out_specs, check_vma=False
    )
```

time: 154 us -> 19.7 us (0.13); the launches traced: 152 us -> 19.5 us
  starting transfers between devices: 77.1 us -> 0 us
  waiting for transfers between devices: 53.3 us -> 0 us
  Pallas kernels: 0 us -> 18.7 us
  other arithmetic: 13.5 us -> 0 us
  local copies, waits for them, and re-layouts: 7.24 us -> 0.8 us
    ppermute x18 -> x0, starting transfers between devices: 77.1 us -> none  [the longest x10 30.4 us: swapped(): lax.ppermute(value, axis, [(i, i ^ 1 << apart) for i in range(lax.axis_si...]
    ppermute x18 -> x0, waiting for transfers between devices: 53.3 us -> none  [the longest x10 26.8 us: swapped(): lax.ppermute(value, axis, [(i, i ^ 1 << apart) for i in range(lax.axis_si...]
    pallas_call x0 -> x1, Pallas kernels: none -> 18.7 us  [local(): pl.pallas_call(functools.partial(kernel, nb, ny), out_shape=vmem((FIELDS...]
    mul x8 -> x0, other arithmetic: 6.5 us -> none  [the longest x2 1.79 us: advance(): 0.5 * zonal_vel * (bound_east - bound_west)]
    unnamed x92 -> x1, local copies, waits for them, and re-layouts: 4.36 us -> 0.8 us
    another operation x3 -> x0, other arithmetic: 1.82 us -> none  [the longest x2 1.45 us: advance(): pressure = jnp.cumsum(density, axis=0)]
  transfers between devices with their start and end apart: 18 -> 0, of which waited for: 12 -> 0; matrix products, arithmetic and copies ran while one was open for 2% -> 0% of each run, Pallas kernels for 0% -> 0%
where the time goes in v1:
time: 19.7 us; the launch traced here: 19.5 us
  Pallas kernels  18.7 us (95%)
  local copies, waits for them, and re-layouts  0.8 us (4%)
    pallas_call x1, Pallas kernels, local(): pl.pallas_call(functools.partial(kernel, nb, ny), out_shape=vmem((FIELDS...  18.7 us
    unnamed x1, local copies, waits for them, and re-layouts  0.8 us

profile of v1, /device:TPU:1, one launch (start us, length us, event | category | flops | bytes accessed | tf_op | source)
XLA Modules:
  0.0 19.5 jit_solution(18207043082798877811)
XLA Ops:
  0.0 18.7 %shard_map.37 = f32[1024,128]{1,0:T(8,128)S(1)} custom-call(f32[1024,128]{1,0:T(8,128)} %bitcast.3, s32[32,128]{1,0:T(8,128)} %level_count.1, f32[32]{0:T(128)} %coriolis.1), custom_call_target="tpu_custom_call" | custom-call | tf_op jit(solution)/shard_map/pallas_call | solution.py:350
  18.7 0.8 %copy.5 = f32[4,8,32,128]{3,2,1,0:T(8,128)} copy(f32[4,8,32,128]{3,2,1,0:T(8,128)S(1)} %bitcast.2) | data formatting | bytes 1048576

commit v2 on v1

--- a/solution.py
+++ b/solution.py
@@ -108,7 +108,7 @@
 def kernel(
     nb, ny, state, level_count, coriolis, out,
     x, y, depth_i, depth, turn_s, turn, tall, packed, ew_out, ns_out, co_out, ew_in, ns_in, co_in,
-    load_sem, send_sem, recv_sem,
+    load_sem, send_sem, recv_sem, go_sem,
 ):
     bx, by = lax.axis_index("bx"), lax.axis_index("by")
     top = by // (ny - 1)
@@ -121,32 +121,61 @@
     south = by - 1
     flip = 1.0 - 2.0 * top.astype(jnp.float32)
 
+    def is_earlier(column, line):
+        half = nb // 2
+        late, other_late = bx >= half, column >= half
+        both_late = jnp.logical_and(late, other_late)
+        beside = jnp.logical_and(line != by, jnp.logical_or(both_late, bx // 2 == column // 2))
+        last, other_last = bx == nb - 1, column == nb - 1
+        corner_last = jnp.logical_and(
+            jnp.logical_and(both_late, line != by), jnp.logical_and(last != other_last, jnp.logical_or(last, other_last)))
+        one_late = late != other_late
+        in_order = jnp.logical_or(
+            jnp.logical_and(one_late, late), jnp.logical_and(jnp.logical_not(one_late), column < bx))
+        first_of_all = jnp.logical_and(jnp.logical_and(bx == 0, by == 0), column == 1)
+        to_first_of_all = jnp.logical_and(jnp.logical_and(column == 0, line == 0), bx == 1)
+        answer = jnp.logical_or(
+            jnp.logical_and(beside, jnp.logical_or(
+                jnp.logical_and(corner_last, other_last),
+                jnp.logical_and(jnp.logical_not(corner_last), line % 2 == 1))),
+            jnp.logical_and(jnp.logical_not(beside), jnp.logical_or(
+                jnp.logical_and(both_late, column % 2 == 0),
+                jnp.logical_and(jnp.logical_not(both_late), in_order))))
+        return jnp.logical_and(jnp.logical_or(answer, first_of_all), jnp.logical_not(to_first_of_all))
+
     ne_to, nw_to = north(east), north(west)
     ne_other = jnp.logical_or(ne_to[0] != bx, ne_to[1] != by)
     nw_other = jnp.logical_or(nw_to[0] != bx, nw_to[1] != by)
+    ne_slot, nw_slot = SW + (NE - SW) * top, SE + (NW - SE) * top
     plan = [
-        (ew_out.at[0], ew_in.at[WEST], WEST, (east, by), None),
-        (ew_out.at[1], ew_in.at[EAST], EAST, (west, by), None),
-        (co_out.at[0], co_in.at[SW + (NE - SW) * top], 4 + SW + (NE - SW) * top, ne_to, ne_other),
-        (co_out.at[1], co_in.at[SE + (NW - SE) * top], 4 + SE + (NW - SE) * top, nw_to, nw_other),
-        (co_out.at[2], co_in.at[NW], 4 + NW, (east, south), has_south),
-        (co_out.at[3], co_in.at[NE], 4 + NE, (west, south), has_south),
-        (ns_out.at[0], ns_in.at[SOUTH + top], 2 + SOUTH + top, north(bx), None),
-        (ns_out.at[1], ns_in.at[NORTH], 2 + NORTH, (bx, south), has_south),
+        (ns_out.at[1], ns_in.at[NORTH], 2 + NORTH, (bx, south), has_south, 2 + SOUTH),
+        (ew_out.at[0], ew_in.at[WEST], WEST, (east, by), None, EAST),
+        (co_out.at[2], co_in.at[NW], 4 + NW, (east, south), has_south, 4 + SE),
+        (ns_out.at[0], ns_in.at[SOUTH + top], 2 + SOUTH + top, north(bx), None, 2 + NORTH),
+        (co_out.at[0], co_in.at[ne_slot], 4 + ne_slot, ne_to, ne_other, 4 + NE),
+        (ew_out.at[1], ew_in.at[EAST], EAST, (west, by), None, WEST),
+        (co_out.at[3], co_in.at[NE], 4 + NE, (west, south), has_south, 4 + SW),
+        (co_out.at[1], co_in.at[nw_slot], 4 + nw_slot, nw_to, nw_other, 4 + NW),
     ]
+    stranger_south = jnp.logical_and(bx == nb - 1, by % 2 == 0)
+    stranger_north = jnp.logical_and(jnp.logical_and(bx == nb - 1, by % 2 == 1), by < ny - 1)
+    introduces = jnp.logical_and(jnp.logical_and(bx == 0, by % 2 == 1), by < ny - 1)
+    before, after, greets = [], [], []
+    for i, (_, _, _, device, condition, _) in enumerate(plan):
+        earlier = is_earlier(*device)
+        if i in (0, 3):
+            stranger = stranger_south if i == 0 else stranger_north
+            earlier = jnp.logical_and(earlier, jnp.logical_not(stranger))
+        later = jnp.logical_not(earlier)
+        before.append(earlier if condition is None else jnp.logical_and(condition, earlier))
+        after.append(later if condition is None else jnp.logical_and(condition, later))
+        greets.append(jnp.logical_and(after[i], jnp.logical_not(stranger)) if i in (0, 3) else after[i])
 
     def when(condition, run):
         if condition is None:
             run()
         else:
             pl.when(condition)(run)
-
-    barrier = pltpu.get_barrier_semaphore()
-    partners = jnp.int32(0)
-    for _, _, _, device, condition in plan:
-        when(condition, functools.partial(
-            pl.semaphore_signal, barrier, inc=1, device_id=device, device_id_type=MESH))
-        partners = partners + (1 if condition is None else condition.astype(jnp.int32))
 
     loads = [
         pltpu.make_async_copy(level_count, depth_i, load_sem.at[FIELDS]),
@@ -159,6 +188,28 @@
     for load in loads:
         load.start()
 
+    barrier = pltpu.get_barrier_semaphore()
+    greetings = jnp.int32(0)
+    for i, (_, _, _, device, _, _) in enumerate(plan):
+        when(greets[i], functools.partial(
+            pl.semaphore_signal, barrier, inc=1, device_id=device, device_id_type=MESH))
+        greetings = greetings + before[i].astype(jnp.int32)
+
+    pl.when(greetings > 0)(functools.partial(pl.semaphore_wait, barrier, greetings))
+    for i, (_, _, slot, device, _, _) in enumerate(plan):
+        when(before[i], functools.partial(
+            pl.semaphore_signal, go_sem.at[slot], inc=1, device_id=device, device_id_type=MESH))
+    copies = [
+        pltpu.make_async_remote_copy(
+            src_ref=source, dst_ref=target, send_sem=send_sem.at[i], recv_sem=recv_sem.at[slot],
+            device_id=device, device_id_type=MESH)
+        for i, (source, target, slot, device, _, _) in enumerate(plan)
+    ]
+
+    def send_to_earlier(*which):
+        for i in which:
+            when(before[i], copies[i].start)
+
     lane = lax.broadcasted_iota(jnp.int32, (LEV, CX), 1)
     level = lax.broadcasted_iota(jnp.int32, (LEV, CX), 0)
     lane_tall = lax.broadcasted_iota(jnp.int32, (CY, CX), 1)
@@ -170,23 +221,38 @@
         co_in[SW] = jnp.zeros((LEV, CX), jnp.float32)
         co_in[SE] = jnp.zeros((LEV, CX), jnp.float32)
 
+    def row(ref, f, r):
+        return ref[pl.ds(f * LEV * CY + r, LEV, stride=CY), :]
+
+    for load in loads:
+        load.wait()
+    depth[...] = depth_i[...].astype(jnp.float32)
+
+    def corner_cells(r):
+        value = jnp.zeros((LEV, CX), jnp.float32)
+        for f in range(FIELDS + 1):
+            line = row(x, f, r) if f < FIELDS else jnp.broadcast_to(depth[pl.ds(r, 1), :], (LEV, CX))
+            value = jnp.where(lane // 4 == f, pltpu.roll(line, 2 + 4 * f, 1), value)
+        return value
+
+    upper, lower = corner_cells(CY - 1), corner_cells(0)
+    upper = upper * jnp.where(jnp.logical_or(lane // 4 == 2, lane // 4 == 3), flip, 1.0)
+    co_out[0] = jnp.where(left, upper, pltpu.roll(upper, 97, 1))
+    co_out[1] = jnp.where(left, pltpu.roll(upper, 32, 1), pltpu.roll(upper, 63, 1))
+    co_out[2] = pltpu.roll(lower, 33, 1)
+    co_out[3] = pltpu.roll(lower, 96, 1)
+    send_to_earlier(4, 2, 7, 6)
+
     def transposed(group, value):
         tall[group, pl.ds(2, CY), :] = value
         tall[group, pl.ds(66, CY), :] = value
         packed[group] = tall[group].T
 
-    for load in loads[:2]:
-        load.wait()
-    depth[...] = depth_i[...].astype(jnp.float32)
-    for r in range(CY):
-        turn[pl.ds(r, 1), :] = jnp.full((1, CX), turn_s[r], jnp.float32)
     transposed(2, pltpu.roll(depth[...], 4, 1))
 
     for group in range(2):
         value = jnp.zeros((CY, CX), jnp.float32)
         for q in range(16):
-            if q % LEV == 0:
-                loads[2 + 2 * group + q // LEV].wait()
             moved = pltpu.roll(x[pl.ds((16 * group + q) * CY, CY), :], (8 * q + 4) % CX, 1)
             value = jnp.where(lane_tall // 8 == q, moved, value)
         transposed(group, value)
@@ -196,31 +262,11 @@
             return jnp.broadcast_to(packed[2, pl.ds(c, 1), :], (LEV, CX))
         return packed[f // 2, pl.ds((f % 2) * 64 + c, LEV, stride=8), :]
 
-    def row(ref, f, r):
-        return ref[pl.ds(f * LEV * CY + r, LEV, stride=CY), :]
-
-    corners = [jnp.zeros((LEV, CX), jnp.float32) for _ in range(4)]
     for f in range(FIELDS + 1):
-        edge_w, edge_e = column(f, 4), column(f, 3)
-        ew_out[0, f] = jnp.where(left, edge_e, column(f, 2))
-        ew_out[1, f] = jnp.where(left, column(f, 5), edge_w)
-        s = 4 * f
-        if f in (2, 3):
-            fold_e, fold_w = edge_e * flip, edge_w * flip
-        else:
-            fold_e, fold_w = edge_e, edge_w
-
-        def put(i, at, value):
-            corners[i] = jnp.where(lane == at + s, value, corners[i])
-
-        put(0, 1, pltpu.roll(fold_e, (96 + s) % CX, 1))
-        put(0, 98, pltpu.roll(fold_e, 1 + s, 1))
-        put(1, 65, pltpu.roll(fold_w, (96 + s) % CX, 1))
-        put(1, 34, pltpu.roll(fold_w, 1 + s, 1))
-        put(2, 34, pltpu.roll(edge_e, 32 + s, 1))
-        put(3, 98, pltpu.roll(edge_w, 32 + s, 1))
-    for i in range(4):
-        co_out[i] = corners[i]
+        ew_out[0, f] = jnp.where(left, column(f, 3), column(f, 2))
+        ew_out[1, f] = jnp.where(left, column(f, 5), column(f, 4))
+
+    send_to_earlier(1, 5)
 
     for side, rows in ((0, (31, 30)), (1, (0, 1))):
         for f in range(FIELDS):
@@ -228,7 +274,7 @@
                 ns_out[side, 2 * f + i] = row(x, f, r)
         ns_out[side, 8] = jnp.where(
             level == 0, depth[pl.ds(rows[0], 1), :],
-            jnp.where(level == 1, depth[pl.ds(rows[1], 1), :], turn[pl.ds(rows[0], 1), :]))
+            jnp.where(level == 1, depth[pl.ds(rows[1], 1), :], turn_s[rows[0]]))
 
     @pl.when(top == 1)
     def _():
@@ -236,14 +282,7 @@
             mirrored = jnp.take_along_axis(ns_out[0, i], (CX - 1) - lane, axis=1)
             ns_out[0, i] = -mirrored if i in (4, 5, 6, 7) else mirrored
 
-    pl.semaphore_wait(barrier, partners)
-    sends = []
-    for i, (source, target, slot, device, condition) in enumerate(plan):
-        copy = pltpu.make_async_remote_copy(
-            src_ref=source, dst_ref=target, send_sem=send_sem.at[i], recv_sem=recv_sem.at[slot],
-            device_id=device, device_id_type=MESH)
-        when(condition, copy.start)
-        sends.append((copy, condition))
+    send_to_earlier(3, 0)
 
     @pl.when(jnp.logical_not(ne_other))
     def _():
@@ -253,8 +292,19 @@
     def _():
         co_in[NW] = co_out[1]
 
+    for r in range(CY):
+        turn[pl.ds(r, 1), :] = jnp.full((1, CX), turn_s[r], jnp.float32)
     block_step(x, y, depth[...], turn[...])
     block_step(y, out, depth[...], turn[...])
+
+    for i, (_, _, _, _, _, here) in enumerate(plan):
+        when(after[i], functools.partial(pl.semaphore_wait, go_sem.at[here], 1))
+        when(after[i], copies[i].start)
+
+    @pl.when(introduces)
+    def _():
+        pl.semaphore_signal(go_sem.at[2 + NORTH], inc=1, device_id=(west, by), device_id_type=MESH)
+        pl.semaphore_signal(go_sem.at[2 + SOUTH], inc=1, device_id=(west, by + 1), device_id_type=MESH)
 
     def received(ref, slot, condition):
         copy = pltpu.make_async_remote_copy(
@@ -340,7 +390,7 @@
         spot = out.at[pl.ds(p * CY, CY)]
         spot[...] = jnp.where(at_edge, moved, spot[...])
 
-    for copy, condition in sends:
+    for copy, (_, _, _, _, condition, _) in zip(copies, plan):
         when(condition, copy.wait_send)
 
 
@@ -370,6 +420,7 @@
             pltpu.SemaphoreType.DMA((FIELDS + 2,)),
             pltpu.SemaphoreType.DMA((8,)),
             pltpu.SemaphoreType.DMA((8,)),
+            pltpu.SemaphoreType.REGULAR((8,)),
         ],
         compiler_params=pltpu.CompilerParams(collective_id=0, has_side_effects=True),
     )(state.reshape(FIELDS * LEV * CY, CX), level_count, coriolis)

time: 19.7 us -> 18.3 us (0.929)
  Pallas kernels: 18.7 us -> 17.2 us
    pallas_call x1, Pallas kernels: 18.7 us -> 17.2 us  [local(): pl.pallas_call(functools.partial(kernel, nb, ny), out_shape=vmem((FIELDS...]
where the time goes in v2:
time: 18.3 us; the launch traced here: 18 us
  Pallas kernels  17.2 us (94%)
  local copies, waits for them, and re-layouts  0.8 us (4%)
    pallas_call x1, Pallas kernels, local(): pl.pallas_call(functools.partial(kernel, nb, ny), out_shape=vmem((FIELDS...  17.2 us
    unnamed x1, local copies, waits for them, and re-layouts  0.8 us

profile of v2, /device:TPU:1, one launch (start us, length us, event | category | flops | bytes accessed | tf_op | source)
XLA Modules:
  0.0 18.0 jit_solution(1834876198208744835)
XLA Ops:
  0.0 17.2 %shard_map.37 = f32[1024,128]{1,0:T(8,128)S(1)} custom-call(f32[1024,128]{1,0:T(8,128)} %bitcast.3, s32[32,128]{1,0:T(8,128)} %level_count.1, f32[32]{0:T(128)} %coriolis.1), custom_call_target="tpu_custom_call" | custom-call | tf_op jit(solution)/shard_map/pallas_call | solution.py:400
  17.2 0.8 %copy.5 = f32[4,8,32,128]{3,2,1,0:T(8,128)} copy(f32[4,8,32,128]{3,2,1,0:T(8,128)S(1)} %bitcast.2) | data formatting | bytes 1048576

commit v3 on v2

v3 whole, which is shorter than its diff:
```python
import functools

import jax
import jax.numpy as jnp
from jax import lax
from jax.experimental import pallas as pl
from jax.experimental.pallas import tpu as pltpu
from jax.sharding import PartitionSpec as P

MESH = pl.DeviceIdType.MESH
FIELDS, LEV, CY, CX = 4, 8, 32, 128
DT = 0.2
COEF = (DT * 0.5, DT * 0.5, DT * 0.4, DT * 0.4)
HALF = DT * 0.5
SOUTH, NORTH = 0, 1
WEST, EAST, SW, NW, SE, NE = 0, 5, 10, 11, 12, 13
SIDES = 14
TO_EAST, TO_WEST, TO_NE, TO_NW, TO_SE, TO_SW, TO_NORTH, TO_SOUTH = 0, 5, 10, 11, 12, 13, 14, 23
SENT = 32
BASE = 8


def update(center, ahead, behind, inner, outer, pressures, masks, along, sign_across, planetary):
    across = 5 - along
    m_c, m_a, m_b, m_i, m_o = masks
    p_c, p_a, p_b, p_i, p_o = pressures
    h_along = HALF * center[along]
    h_across = sign_across * (HALF * center[across])
    grad_along = HALF * (jnp.where(m_a, p_a, p_c) - jnp.where(m_b, p_b, p_c))
    grad_across = sign_across * (HALF * (jnp.where(m_i, p_i, p_c) - jnp.where(m_o, p_o, p_c)))
    grad = {along: grad_along, across: grad_across}
    turn = DT * planetary
    force = {2: turn * center[3] - grad[2], 3: -turn * center[2] - grad[3]}
    result = []
    for f in range(FIELDS):
        c = center[f]
        b_a, b_b = jnp.where(m_a, ahead[f], c), jnp.where(m_b, behind[f], c)
        b_i, b_o = jnp.where(m_i, inner[f], c), jnp.where(m_o, outer[f], c)
        new = (1.0 - 4.0 * COEF[f]) * c + COEF[f] * ((b_a + b_b) + (b_i + b_o))
        new = new - h_along * (b_a - b_b) - h_across * (b_i - b_o)
        if f >= 2:
            new = new + force[f]
        result.append(jnp.where(m_c, new, 0.0))
    return result


class Line:
    def __init__(self, fields, depth, turn=None, whole=True):
        level = lax.broadcasted_iota(jnp.int32, (LEV, CX), 0)
        level_f = level.astype(jnp.float32)
        self.fields, self.turn = fields, turn
        self.mask = level_f < depth
        total = jnp.where(self.mask, 0.4 * fields[1] - 0.5 * fields[0], 0.0)
        for shift in (1, 2, 4):
            total = total + jnp.where(level >= shift, pltpu.roll(total, shift, 0), 0.0)
        self.pressure = total
        if whole:
            self.around = [
                ([pltpu.roll(x, shift, 1) for x in fields], level_f < pltpu.roll(depth, shift, 1), pltpu.roll(total, shift, 1))
                for shift in (CX - 1, 1)
            ]

    def step(self, inner, outer, along, sign_across):
        (ahead, m_a, p_a), (behind, m_b, p_b) = self.around
        return update(
            self.fields, ahead, behind, inner.fields, outer.fields,
            (self.pressure, p_a, p_b, inner.pressure, outer.pressure),
            (self.mask, m_a, m_b, inner.mask, outer.mask), along, sign_across, self.turn)


def block_step(src, dst, depth, planetary):
    d_e, d_w = pltpu.roll(depth, CX - 1, 1), pltpu.roll(depth, 1, 1)
    d_n, d_s = pltpu.roll(depth, CY - 1, 0), pltpu.roll(depth, 1, 0)

    def level_step(k, p):
        kf = k.astype(jnp.float32)
        center = [src[pl.ds(pl.multiple_of(f * LEV * CY + k * CY, CY), CY), :] for f in range(FIELDS)]
        masks = [kf < d for d in (depth, d_e, d_w, d_n, d_s)]
        p = p + jnp.where(masks[0], 0.4 * center[1] - 0.5 * center[0], 0.0)

        def moved(x):
            return (pltpu.roll(x, CX - 1, 1), pltpu.roll(x, 1, 1), pltpu.roll(x, CY - 1, 0), pltpu.roll(x, 1, 0))

        around = [moved(x) for x in center]
        new = update(
            center, *[[a[i] for a in around] for i in range(4)], (p, *moved(p)), masks, 2, 1.0, planetary
        )
        for f in range(FIELDS):
            dst[pl.ds(pl.multiple_of(f * LEV * CY + k * CY, CY), CY), :] = new[f]
        return p

    lax.fori_loop(0, LEV, level_step, jnp.zeros((CY, CX), jnp.float32))


def kernel(
    nb, ny, state, level_count, coriolis, out,
    x, y, depth_i, depth, turn_s, turn, tall, packed, sent, sides, rows_in,
    load_sem, send_sem, recv_sem, go_sem,
):
    bx, by = lax.axis_index("bx"), lax.axis_index("by")
    loads = [
        pltpu.make_async_copy(state, x, load_sem.at[0]),
        pltpu.make_async_copy(level_count, depth_i, load_sem.at[1]),
        pltpu.make_async_copy(coriolis, turn_s, load_sem.at[2]),
    ]
    for load in loads:
        load.start()

    top = by // (ny - 1)
    east, west = lax.rem(bx + 1, nb), lax.rem(bx + nb - 1, nb)

    def north(column):
        return column + top * (nb - 1 - 2 * column), by + 1 - top

    has_south = by > 0
    south = by - 1
    flip = 1.0 - 2.0 * top.astype(jnp.float32)

    def is_earlier(column, line):
        half = nb // 2
        late, other_late = bx >= half, column >= half
        both_late = jnp.logical_and(late, other_late)
        beside = jnp.logical_and(line != by, jnp.logical_or(both_late, bx // 2 == column // 2))
        last, other_last = bx == nb - 1, column == nb - 1
        corner_last = jnp.logical_and(
            jnp.logical_and(both_late, line != by), jnp.logical_and(last != other_last, jnp.logical_or(last, other_last)))
        one_late = late != other_late
        in_order = jnp.logical_or(
            jnp.logical_and(one_late, late), jnp.logical_and(jnp.logical_not(one_late), column < bx))
        first_of_all = jnp.logical_and(jnp.logical_and(bx == 0, by == 0), column == 1)
        to_first_of_all = jnp.logical_and(jnp.logical_and(column == 0, line == 0), bx == 1)
        answer = jnp.logical_or(
            jnp.logical_and(beside, jnp.logical_or(
                jnp.logical_and(corner_last, other_last),
                jnp.logical_and(jnp.logical_not(corner_last), line % 2 == 1))),
            jnp.logical_and(jnp.logical_not(beside), jnp.logical_or(
                jnp.logical_and(both_late, column % 2 == 0),
                jnp.logical_and(jnp.logical_not(both_late), in_order))))
        return jnp.logical_and(jnp.logical_or(answer, first_of_all), jnp.logical_not(to_first_of_all))

    ne_to, nw_to = north(east), north(west)
    ne_other = jnp.logical_or(ne_to[0] != bx, ne_to[1] != by)
    nw_other = jnp.logical_or(nw_to[0] != bx, nw_to[1] != by)
    plan = [
        (TO_SOUTH, 9, rows_in.at[NORTH], NORTH, (bx, south), has_south, 0),
        (TO_EAST, 5, sides.at[pl.ds(WEST, 5)], 2, (east, by), None, 1),
        (TO_SE, 1, sides.at[pl.ds(NW, 1)], 2, (east, south), has_south, 1),
        (TO_NORTH, 9, rows_in.at[SOUTH + top], SOUTH + top, north(bx), None, top),
        (TO_NE, 1, sides.at[pl.ds(SW + (NE - SW) * top, 1)], 2, ne_to, ne_other, 1),
        (TO_WEST, 5, sides.at[pl.ds(EAST, 5)], 2, (west, by), None, 0),
        (TO_SW, 1, sides.at[pl.ds(NE, 1)], 2, (west, south), has_south, 0),
        (TO_NW, 1, sides.at[pl.ds(SE + (NW - SE) * top, 1)], 2, nw_to, nw_other, top),
    ]
    groups = (0, 0, 0, top, top, 1, 1, 1)

    stranger_south = jnp.logical_and(bx == nb - 1, by % 2 == 0)
    stranger_north = jnp.logical_and(jnp.logical_and(bx == nb - 1, by % 2 == 1), by < ny - 1)
    introduces = jnp.logical_and(jnp.logical_and(bx == 0, by % 2 == 1), by < ny - 1)
    before, after, greets = [], [], []
    for i, (_, _, _, _, device, condition, _) in enumerate(plan):
        earlier = is_earlier(*device)
        if i in (0, 3):
            stranger = stranger_south if i == 0 else stranger_north
            earlier = jnp.logical_and(earlier, jnp.logical_not(stranger))
        later = jnp.logical_not(earlier)
        before.append(earlier if condition is None else jnp.logical_and(condition, earlier))
        after.append(later if condition is None else jnp.logical_and(condition, later))
        greets.append(jnp.logical_and(after[i], jnp.logical_not(stranger)) if i in (0, 3) else after[i])

    def signal(semaphore, device):
        pl.semaphore_signal(semaphore, inc=1, device_id=device, device_id_type=MESH)

    barrier = pltpu.get_barrier_semaphore()
    greetings = jnp.int32(0)
    answers = [jnp.int32(0), jnp.int32(0)]
    for i, (_, _, _, _, device, _, _) in enumerate(plan):
        pl.when(greets[i])(functools.partial(signal, barrier, device))
        greetings = greetings + before[i].astype(jnp.int32)
        counted = after[i].astype(jnp.int32)
        answers[0] = answers[0] + counted * (1 - groups[i])
        answers[1] = answers[1] + counted * groups[i]
    pl.when(greetings > 0)(functools.partial(pl.semaphore_wait, barrier, greetings))
    for i, (_, _, _, _, device, _, group) in enumerate(plan):
        pl.when(before[i])(functools.partial(signal, go_sem.at[group], device))
    copies = [
        pltpu.make_async_remote_copy(
            src_ref=sent.at[pl.ds(first, tiles)], dst_ref=target, send_sem=send_sem, recv_sem=recv_sem.at[slot],
            device_id=device, device_id_type=MESH)
        for first, tiles, target, slot, device, _, _ in plan
    ]

    def send_to_earlier(*which):
        for i in which:
            pl.when(before[i])(copies[i].start)

    lane = lax.broadcasted_iota(jnp.int32, (LEV, CX), 1)
    level = lax.broadcasted_iota(jnp.int32, (LEV, CX), 0)
    lane_tall = lax.broadcasted_iota(jnp.int32, (CY, CX), 1)
    left = lane < 64

    @pl.when(jnp.logical_not(has_south))
    def _():
        rows_in[SOUTH] = jnp.zeros((9, LEV, CX), jnp.float32)
        sides[SW] = jnp.zeros((LEV, CX), jnp.float32)
        sides[SE] = jnp.zeros((LEV, CX), jnp.float32)

    def row(ref, f, r):
        return ref[pl.ds(f * LEV * CY + r, LEV, stride=CY), :]

    for load in loads:
        load.wait()
    depth[...] = depth_i[...].astype(jnp.float32)

    def corner_cells(r):
        value = jnp.zeros((LEV, CX), jnp.float32)
        for f in range(FIELDS + 1):
            line = row(x, f, r) if f < FIELDS else jnp.broadcast_to(depth[pl.ds(r, 1), :], (LEV, CX))
            value = jnp.where((lane + 1) // 4 == f + 2, pltpu.roll(line, BASE + 4 * f, 1), value)
        return value

    upper, lower = corner_cells(CY - 1), corner_cells(0)
    upper = upper * jnp.where((lane + 1) // 8 == 2, flip, 1.0)
    sent[TO_NE] = jnp.where(left, upper, pltpu.roll(upper, 97, 1))
    sent[TO_NW] = jnp.where(left, pltpu.roll(upper, 32, 1), pltpu.roll(upper, 63, 1))
    sent[TO_SE] = pltpu.roll(lower, 33, 1)
    sent[TO_SW] = pltpu.roll(lower, 96, 1)
    send_to_earlier(4, 2, 7, 6)

    for side, rows in ((TO_NORTH, (31, 30)), (TO_SOUTH, (0, 1))):
        for f in range(FIELDS):
            for i, r in enumerate(rows):
                sent[side + 2 * f + i] = row(x, f, r)
        sent[side + 8] = jnp.where(
            level == 0, depth[pl.ds(rows[0], 1), :],
            jnp.where(level == 1, depth[pl.ds(rows[1], 1), :], turn_s[rows[0]]))

    @pl.when(top == 1)
    def _():
        for i in range(9):
            mirrored = jnp.take_along_axis(sent[TO_NORTH + i], (CX - 1) - lane, axis=1)
            sent[TO_NORTH + i] = -mirrored if i in (4, 5, 6, 7) else mirrored

    def transposed(group, value):
        tall[group, pl.ds(BASE, CY), :] = value
        tall[group, pl.ds(64 + BASE, CY), :] = value
        packed[group] = tall[group].T

    transposed(2, pltpu.roll(depth[...], 4, 1))
    for group in range(2):
        value = jnp.zeros((CY, CX), jnp.float32)
        for q in range(16):
            moved = pltpu.roll(x[pl.ds((16 * group + q) * CY, CY), :], (8 * q + 4) % CX, 1)
            value = jnp.where(lane_tall // 8 == q, moved, value)
        transposed(group, value)

    def column(f, c):
        if f == FIELDS:
            return jnp.broadcast_to(packed[2, pl.ds(c, 1), :], (LEV, CX))
        return packed[f // 2, pl.ds((f % 2) * 64 + c, LEV, stride=8), :]

    for f in range(FIELDS + 1):
        sent[TO_EAST + f] = jnp.where(left, column(f, 3), column(f, 2))
        sent[TO_WEST + f] = jnp.where(left, column(f, 5), column(f, 4))
    send_to_earlier(1, 5)
    send_to_earlier(3, 0)

    @pl.when(jnp.logical_not(ne_other))
    def _():
        sides[NE] = sent[TO_NE]

    @pl.when(jnp.logical_not(nw_other))
    def _():
        sides[NW] = sent[TO_NW]

    for r in range(CY):
        turn[pl.ds(r, 1), :] = jnp.full((1, CX), turn_s[r], jnp.float32)
    block_step(x, y, depth[...], turn[...])
    block_step(y, out, depth[...], turn[...])

    for group in range(2):
        pl.when(answers[group] > 0)(functools.partial(pl.semaphore_wait, go_sem.at[group], answers[group]))
        for i in range(8):
            if isinstance(groups[i], int):
                if groups[i] == group:
                    pl.when(after[i])(copies[i].start)
            else:
                pl.when(jnp.logical_and(after[i], groups[i] == group))(copies[i].start)

    @pl.when(introduces)
    def _():
        signal(go_sem.at[0], (west, by))
        signal(go_sem.at[0], (west, by + 1))

    def wait_received(ref, slot):
        pltpu.make_async_remote_copy(
            src_ref=ref, dst_ref=ref, send_sem=send_sem, recv_sem=recv_sem.at[slot],
            device_id=(east, by), device_id_type=MESH).wait_recv()

    def spread(ref, r):
        return jnp.broadcast_to(ref[pl.ds(r, 1), :], (LEV, CX))

    def from_halo(side, f, i):
        if f == FIELDS:
            return jnp.broadcast_to(rows_in[side, 8, pl.ds(i, 1), :], (LEV, CX))
        return rows_in[side, 2 * f + i]

    def edge_rows(side, rows, sign):
        depths = [spread(depth, r) for r in rows]
        turns = [spread(turn, r) for r in rows]
        far = Line([from_halo(side, f, 1) for f in range(FIELDS)], from_halo(side, FIELDS, 1), whole=False)
        near = Line([from_halo(side, f, 0) for f in range(FIELDS)], from_halo(side, FIELDS, 0), from_halo(side, FIELDS, 2))
        zero = Line([row(x, f, rows[0]) for f in range(FIELDS)], depths[0], turns[0])
        one = Line([row(x, f, rows[1]) for f in range(FIELDS)], depths[1], whole=False)
        next_near = Line(near.step(zero, far, 2, sign), from_halo(side, FIELDS, 0), whole=False)
        next_zero = Line(zero.step(one, near, 2, sign), depths[0], turns[0])
        next_one = Line([row(y, f, rows[1]) for f in range(FIELDS)], depths[1], turns[1])
        next_two = Line([row(y, f, rows[2]) for f in range(FIELDS)], depths[2], whole=False)
        for r, result in (
            (rows[0], next_zero.step(next_one, next_near, 2, sign)),
            (rows[1], next_one.step(next_two, next_zero, 2, sign)),
        ):
            for f in range(FIELDS):
                out[pl.ds(f * LEV * CY + r, LEV, stride=CY), :] = result[f]

    pl.when(has_south)(functools.partial(wait_received, rows_in.at[SOUTH], SOUTH))
    edge_rows(SOUTH, (0, 1, 2), 1.0)
    wait_received(rows_in.at[NORTH], NORTH)
    edge_rows(NORTH, (31, 30, 29), -1.0)

    def at_rows(j, f):
        value = jnp.where(left, column(f, 4 + j), column(f, 3 - j))
        if j == 3:
            return value
        for side, i, r in ((SOUTH, 0, -1), (SOUTH, 1, -2), (NORTH, 0, CY), (NORTH, 1, CY + 1)):
            if j == 2 and i == 1:
                continue
            halo = from_halo(side, f, i)
            halo = jnp.where(left, halo[:, j : j + 1], halo[:, CX - 1 - j : CX - j])
            value = jnp.where(lane % 64 == BASE + r, halo, value)
        return value

    planetary = jnp.where(lane % 64 == BASE - 1, from_halo(SOUTH, FIELDS, 2), from_halo(NORTH, FIELDS, 2))
    for r in range(CY):
        planetary = jnp.where(lane % 64 == BASE + r, turn_s[r], planetary)
    sign = jnp.where(left, 1.0, -1.0)
    depths = [at_rows(j, FIELDS) for j in range(4)]
    lines = [Line([at_rows(j, f) for f in range(FIELDS)], depths[j], planetary, j < 3) for j in range(4)]
    next_one = Line(lines[1].step(lines[2], lines[0], 3, sign), depths[1], planetary)
    next_two = Line(lines[2].step(lines[3], lines[1], 3, sign), depths[2], whole=False)

    all_other = jnp.logical_and(ne_other, nw_other)
    for condition, tiles in (
        (jnp.logical_and(has_south, all_other), SIDES),
        (jnp.logical_not(has_south), SIDES - 2),
        (jnp.logical_not(all_other), SIDES - 1),
    ):
        pl.when(condition)(functools.partial(wait_received, sides.at[pl.ds(0, tiles)], 2))

    corner = jnp.where(
        left, jnp.where(lane < 32, sides[SW], sides[NW]), jnp.where(lane < 96, sides[SE], sides[NE]))
    at_corner = jnp.logical_or(lane % 64 == BASE - 1, lane % 64 == BASE + CY)

    def outside(f):
        near = jnp.where(left, sides[WEST + f], sides[EAST + f])
        far = jnp.where(left, sides[EAST + f], sides[WEST + f])
        shifted = corner if f == 0 else pltpu.roll(corner, CX - 4 * f, 1)
        return jnp.where(at_corner, shifted, near), pltpu.roll(far, 64, 1)

    beyond = [outside(f) for f in range(FIELDS + 1)]
    far = Line([beyond[f][1] for f in range(FIELDS)], beyond[FIELDS][1], whole=False)
    near = Line([beyond[f][0] for f in range(FIELDS)], beyond[FIELDS][0], planetary)
    next_near = Line(near.step(lines[0], far, 3, sign), beyond[FIELDS][0], whole=False)
    next_zero = Line(lines[0].step(lines[1], near, 3, sign), depths[0], planetary)
    second = (next_zero.step(next_one, next_near, 3, sign), next_one.step(next_two, next_zero, 3, sign))

    for f in range(FIELDS):
        for c, j in ((0, 1), (1, 0), (2, 0), (3, 1)):
            packed[0, pl.ds(f * 32 + c, LEV, stride=4), :] = second[j][f]
    cells = packed[0].T
    edges = jnp.where(lane_tall % 4 >= 2, cells[BASE : BASE + CY], cells[64 + BASE : 64 + BASE + CY])
    at_edge = jnp.logical_or(lane_tall < 2, lane_tall >= CX - 2)
    for p in range(FIELDS * LEV):
        spot = out.at[pl.ds(p * CY, CY)]
        spot[...] = jnp.where(at_edge, pltpu.roll(edges, (126 - 4 * p) % CX, 1), spot[...])

    def wait_sent(tiles):
        ref = sent.at[pl.ds(0, tiles)]
        pltpu.make_async_remote_copy(
            src_ref=ref, dst_ref=ref, send_sem=send_sem, recv_sem=recv_sem.at[2],
            device_id=(east, by), device_id_type=MESH).wait_send()

    for condition, tiles in (
        (jnp.logical_and(has_south, all_other), SENT),
        (jnp.logical_not(has_south), SENT - 11),
        (jnp.logical_not(all_other), SENT - 1),
    ):
        pl.when(condition)(functools.partial(wait_sent, tiles))


def local(nb, ny, state, level_count, coriolis):
    vmem = pltpu.VMEM
    f32 = jnp.float32
    result = pl.pallas_call(
        functools.partial(kernel, nb, ny),
        out_shape=vmem((FIELDS * LEV * CY, CX), f32),
        in_specs=[pl.BlockSpec(memory_space=pltpu.HBM)] * 3,
        out_specs=pl.BlockSpec(memory_space=pltpu.VMEM),
        scratch_shapes=[
            vmem((FIELDS * LEV * CY, CX), f32),
            vmem((FIELDS * LEV * CY, CX), f32),
            vmem((CY, CX), jnp.int32),
            vmem((CY, CX), f32),
            pltpu.SMEM((CY,), f32),
            vmem((CY, CX), f32),
            vmem((3, CX, CX), f32),
            vmem((3, CX, CX), f32),
            vmem((SENT, LEV, CX), f32),
            vmem((SIDES, LEV, CX), f32),
            vmem((2, 9, LEV, CX), f32),
            pltpu.SemaphoreType.DMA((3,)),
            pltpu.SemaphoreType.DMA,
            pltpu.SemaphoreType.DMA((3,)),
            pltpu.SemaphoreType.REGULAR((2,)),
        ],
        compiler_params=pltpu.CompilerParams(collective_id=0, has_side_effects=True),
    )(state.reshape(FIELDS * LEV * CY, CX), level_count, coriolis)
    return result.reshape(FIELDS, LEV, CY, CX)


def solution(mesh):
    nb, ny = mesh.shape["bx"], mesh.shape["by"]
    in_specs = (P(None, None, "by", "bx"), P("by", "bx"), P("by"))
    out_specs = P(None, None, "by", "bx")
    return jax.shard_map(
        functools.partial(local, nb, ny), mesh=mesh, in_specs=in_specs, out_specs=out_specs, check_vma=False
    )
```

time: 18.3 us -> 17.6 us (0.962); the launches traced: 18 us -> 17.4 us
  Pallas kernels: 17.2 us -> 16.6 us
    pallas_call x1, Pallas kernels: 17.2 us -> 16.6 us  [local(): pl.pallas_call(functools.partial(kernel, nb, ny), out_shape=vmem((FIELDS...]
where the time goes in v3:
time: 17.6 us; the launch traced here: 17.4 us
  Pallas kernels  16.6 us (94%)
  local copies, waits for them, and re-layouts  0.8 us (5%)
    pallas_call x1, Pallas kernels, local(): pl.pallas_call(functools.partial(kernel, nb, ny), out_shape=vmem((FIELDS...  16.6 us
    unnamed x1, local copies, waits for them, and re-layouts  0.8 us

profile of v3, /device:TPU:1, one launch (start us, length us, event | category | flops | bytes accessed | tf_op | source)
XLA Modules:
  0.0 17.4 jit_solution(2083198315616481043)
XLA Ops:
  0.0 16.6 %shard_map.37 = f32[1024,128]{1,0:T(8,128)S(1)} custom-call(f32[1024,128]{1,0:T(8,128)} %bitcast.3, s32[32,128]{1,0:T(8,128)} %level_count.1, f32[32]{0:T(128)} %coriolis.1), custom_call_target="tpu_custom_call" | custom-call | tf_op jit(solution)/shard_map/pallas_call | solution.py:403
  16.7 0.8 %copy.5 = f32[4,8,32,128]{3,2,1,0:T(8,128)} copy(f32[4,8,32,128]{3,2,1,0:T(8,128)S(1)} %bitcast.2) | data formatting | bytes 1048576

commit v4 on v3

--- a/solution.py
+++ b/solution.py
@@ -13,10 +13,10 @@
 COEF = (DT * 0.5, DT * 0.5, DT * 0.4, DT * 0.4)
 HALF = DT * 0.5
 SOUTH, NORTH = 0, 1
-WEST, EAST, SW, NW, SE, NE = 0, 5, 10, 11, 12, 13
-SIDES = 14
-TO_EAST, TO_WEST, TO_NE, TO_NW, TO_SE, TO_SW, TO_NORTH, TO_SOUTH = 0, 5, 10, 11, 12, 13, 14, 23
-SENT = 32
+WEST, EAST, SW, NW, SE, NE = 0, 3, 6, 7, 8, 9
+SIDES = 10
+TO_EAST, TO_WEST, TO_NE, TO_NW, TO_SE, TO_SW, TO_NORTH, TO_SOUTH = 0, 3, 6, 7, 8, 9, 10, 19
+SENT = 28
 BASE = 8
 
 
@@ -93,17 +93,21 @@
 
 
 def kernel(
-    nb, ny, state, level_count, coriolis, out,
-    x, y, depth_i, depth, turn_s, turn, tall, packed, sent, sides, rows_in,
+    nb, ny, state, planes, level_count, coriolis, out,
+    x, y, tips, depth_i, depth, turn_s, turn, tall, packed, sent, sides, rows_in,
     load_sem, send_sem, recv_sem, go_sem,
 ):
     bx, by = lax.axis_index("bx"), lax.axis_index("by")
+    tip_loads = [
+        pltpu.make_async_copy(planes.at[:, r, :], tips.at[pl.ds(i * FIELDS * LEV, FIELDS * LEV)], load_sem.at[3])
+        for i, r in enumerate((CY - 1, 0))
+    ]
     loads = [
+        pltpu.make_async_copy(level_count, depth_i, load_sem.at[1]),
         pltpu.make_async_copy(state, x, load_sem.at[0]),
-        pltpu.make_async_copy(level_count, depth_i, load_sem.at[1]),
         pltpu.make_async_copy(coriolis, turn_s, load_sem.at[2]),
     ]
-    for load in loads:
+    for load in tip_loads + loads:
         load.start()
 
     top = by // (ny - 1)
@@ -134,7 +138,8 @@
                 jnp.logical_and(corner_last, other_last),
                 jnp.logical_and(jnp.logical_not(corner_last), line % 2 == 1))),
             jnp.logical_and(jnp.logical_not(beside), jnp.logical_or(
-                jnp.logical_and(both_late, column % 2 == 0),
+                jnp.logical_and(both_late, jnp.logical_or(
+                    other_last, jnp.logical_and(column % 2 == 0, jnp.logical_not(last)))),
                 jnp.logical_and(jnp.logical_not(both_late), in_order))))
         return jnp.logical_and(jnp.logical_or(answer, first_of_all), jnp.logical_not(to_first_of_all))
 
@@ -143,11 +148,11 @@
     nw_other = jnp.logical_or(nw_to[0] != bx, nw_to[1] != by)
     plan = [
         (TO_SOUTH, 9, rows_in.at[NORTH], NORTH, (bx, south), has_south, 0),
-        (TO_EAST, 5, sides.at[pl.ds(WEST, 5)], 2, (east, by), None, 1),
+        (TO_EAST, 3, sides.at[pl.ds(WEST, 3)], 2, (east, by), None, 1),
         (TO_SE, 1, sides.at[pl.ds(NW, 1)], 2, (east, south), has_south, 1),
         (TO_NORTH, 9, rows_in.at[SOUTH + top], SOUTH + top, north(bx), None, top),
         (TO_NE, 1, sides.at[pl.ds(SW + (NE - SW) * top, 1)], 2, ne_to, ne_other, 1),
-        (TO_WEST, 5, sides.at[pl.ds(EAST, 5)], 2, (west, by), None, 0),
+        (TO_WEST, 3, sides.at[pl.ds(EAST, 3)], 2, (west, by), None, 0),
         (TO_SW, 1, sides.at[pl.ds(NE, 1)], 2, (west, south), has_south, 0),
         (TO_NW, 1, sides.at[pl.ds(SE + (NW - SE) * top, 1)], 2, nw_to, nw_other, top),
     ]
@@ -207,18 +212,21 @@
     def row(ref, f, r):
         return ref[pl.ds(f * LEV * CY + r, LEV, stride=CY), :]
 
-    for load in loads:
-        load.wait()
+    loads[0].wait()
+    pltpu.make_async_copy(tips, tips, load_sem.at[3]).wait()
     depth[...] = depth_i[...].astype(jnp.float32)
 
-    def corner_cells(r):
+    def corner_cells(i, r):
         value = jnp.zeros((LEV, CX), jnp.float32)
         for f in range(FIELDS + 1):
-            line = row(x, f, r) if f < FIELDS else jnp.broadcast_to(depth[pl.ds(r, 1), :], (LEV, CX))
+            if f < FIELDS:
+                line = tips[pl.ds((i * FIELDS + f) * LEV, LEV), :]
+            else:
+                line = jnp.broadcast_to(depth[pl.ds(r, 1), :], (LEV, CX))
             value = jnp.where((lane + 1) // 4 == f + 2, pltpu.roll(line, BASE + 4 * f, 1), value)
         return value
 
-    upper, lower = corner_cells(CY - 1), corner_cells(0)
+    upper, lower = corner_cells(0, CY - 1), corner_cells(1, 0)
     upper = upper * jnp.where((lane + 1) // 8 == 2, flip, 1.0)
     sent[TO_NE] = jnp.where(left, upper, pltpu.roll(upper, 97, 1))
     sent[TO_NW] = jnp.where(left, pltpu.roll(upper, 32, 1), pltpu.roll(upper, 63, 1))
@@ -226,6 +234,8 @@
     sent[TO_SW] = pltpu.roll(lower, 96, 1)
     send_to_earlier(4, 2, 7, 6)
 
+    for load in loads[1:]:
+        load.wait()
     for side, rows in ((TO_NORTH, (31, 30)), (TO_SOUTH, (0, 1))):
         for f in range(FIELDS):
             for i, r in enumerate(rows):
@@ -258,9 +268,14 @@
             return jnp.broadcast_to(packed[2, pl.ds(c, 1), :], (LEV, CX))
         return packed[f // 2, pl.ds((f % 2) * 64 + c, LEV, stride=8), :]
 
-    for f in range(FIELDS + 1):
-        sent[TO_EAST + f] = jnp.where(left, column(f, 3), column(f, 2))
-        sent[TO_WEST + f] = jnp.where(left, column(f, 5), column(f, 4))
+    def side_columns(first, near, far):
+        both = [jnp.where(left, column(f, near), column(f, far)) for f in range(FIELDS + 1)]
+        for i in range(2):
+            sent[first + i] = jnp.where((lane - BASE) % 64 < CY, both[2 * i], pltpu.roll(both[2 * i + 1], CY, 1))
+        sent[first + 2] = both[FIELDS]
+
+    side_columns(TO_EAST, 3, 2)
+    side_columns(TO_WEST, 5, 4)
     send_to_earlier(1, 5)
     send_to_earlier(3, 0)
 
@@ -361,10 +376,15 @@
     at_corner = jnp.logical_or(lane % 64 == BASE - 1, lane % 64 == BASE + CY)
 
     def outside(f):
-        near = jnp.where(left, sides[WEST + f], sides[EAST + f])
-        far = jnp.where(left, sides[EAST + f], sides[WEST + f])
+        shift = CY if f in (1, 3) else 0
+        west_tile, east_tile = sides[WEST + f // 2], sides[EAST + f // 2]
+        west_lanes = (lane + (CX - shift)) % CX < 64
+        near = jnp.where(west_lanes, west_tile, east_tile)
+        far = jnp.where(west_lanes, east_tile, west_tile)
+        if shift:
+            near = pltpu.roll(near, CX - shift, 1)
         shifted = corner if f == 0 else pltpu.roll(corner, CX - 4 * f, 1)
-        return jnp.where(at_corner, shifted, near), pltpu.roll(far, 64, 1)
+        return jnp.where(at_corner, shifted, near), pltpu.roll(far, 64 - shift, 1)
 
     beyond = [outside(f) for f in range(FIELDS + 1)]
     far = Line([beyond[f][1] for f in range(FIELDS)], beyond[FIELDS][1], whole=False)
@@ -403,11 +423,12 @@
     result = pl.pallas_call(
         functools.partial(kernel, nb, ny),
         out_shape=vmem((FIELDS * LEV * CY, CX), f32),
-        in_specs=[pl.BlockSpec(memory_space=pltpu.HBM)] * 3,
+        in_specs=[pl.BlockSpec(memory_space=pltpu.HBM)] * 4,
         out_specs=pl.BlockSpec(memory_space=pltpu.VMEM),
         scratch_shapes=[
             vmem((FIELDS * LEV * CY, CX), f32),
             vmem((FIELDS * LEV * CY, CX), f32),
+            vmem((2 * FIELDS * LEV, CX), f32),
             vmem((CY, CX), jnp.int32),
             vmem((CY, CX), f32),
             pltpu.SMEM((CY,), f32),
@@ -417,13 +438,13 @@
             vmem((SENT, LEV, CX), f32),
             vmem((SIDES, LEV, CX), f32),
             vmem((2, 9, LEV, CX), f32),
-            pltpu.SemaphoreType.DMA((3,)),
+            pltpu.SemaphoreType.DMA((4,)),
             pltpu.SemaphoreType.DMA,
             pltpu.SemaphoreType.DMA((3,)),
             pltpu.SemaphoreType.REGULAR((2,)),
         ],
         compiler_params=pltpu.CompilerParams(collective_id=0, has_side_effects=True),
-    )(state.reshape(FIELDS * LEV * CY, CX), level_count, coriolis)
+    )(state.reshape(FIELDS * LEV * CY, CX), state.reshape(FIELDS * LEV, CY, CX), level_count, coriolis)
     return result.reshape(FIELDS, LEV, CY, CX)
 
 

time: 17.6 us -> 17.2 us (0.977)
  Pallas kernels: 16.6 us -> 16.3 us
    pallas_call x1, Pallas kernels: 16.6 us -> 16.3 us  [local(): pl.pallas_call(functools.partial(kernel, nb, ny), out_shape=vmem((FIELDS...]
where the time goes in v4:
time: 17.2 us; the launch traced here: 17.1 us
  Pallas kernels  16.3 us (95%)
  local copies, waits for them, and re-layouts  0.8 us (5%)
    pallas_call x1, Pallas kernels, local(): pl.pallas_call(functools.partial(kernel, nb, ny), out_shape=vmem((FIELDS...  16.3 us
    unnamed x1, local copies, waits for them, and re-layouts  0.8 us

profile of v4, /device:TPU:1, one launch (start us, length us, event | category | flops | bytes accessed | tf_op | source)
XLA Modules:
  0.0 17.1 jit_solution(15520252444564925936)
XLA Ops:
  0.0 16.3 %shard_map.37 = f32[1024,128]{1,0:T(8,128)S(1)} custom-call(f32[1024,128]{1,0:T(8,128)} %bitcast.4, f32[32,32,128]{2,1,0:T(8,128)} %bitcast.5, s32[32,128]{1,0:T(8,128)} %level_count.1, f32[32]{0:T(128)} %coriolis.1), custom_call_target="tpu_custom_call" | custom-call | tf_op jit(solution)/shard_map/pallas_call | solution.py:423
  16.3 0.8 %copy.5 = f32[4,8,32,128]{3,2,1,0:T(8,128)} copy(f32[4,8,32,128]{3,2,1,0:T(8,128)S(1)} %bitcast.3) | data formatting | bytes 1048576

commit v5 on v4

--- a/solution.py
+++ b/solution.py
@@ -126,8 +126,9 @@
         both_late = jnp.logical_and(late, other_late)
         beside = jnp.logical_and(line != by, jnp.logical_or(both_late, bx // 2 == column // 2))
         last, other_last = bx == nb - 1, column == nb - 1
+        below_top = jnp.logical_and(by < ny - 1, line < ny - 1)
         corner_last = jnp.logical_and(
-            jnp.logical_and(both_late, line != by), jnp.logical_and(last != other_last, jnp.logical_or(last, other_last)))
+            jnp.logical_and(both_late, below_top), jnp.logical_and(line != by, last != other_last))
         one_late = late != other_late
         in_order = jnp.logical_or(
             jnp.logical_and(one_late, late), jnp.logical_and(jnp.logical_not(one_late), column < bx))
@@ -149,28 +150,32 @@
     plan = [
         (TO_SOUTH, 9, rows_in.at[NORTH], NORTH, (bx, south), has_south, 0),
         (TO_EAST, 3, sides.at[pl.ds(WEST, 3)], 2, (east, by), None, 1),
-        (TO_SE, 1, sides.at[pl.ds(NW, 1)], 2, (east, south), has_south, 1),
+        (TO_SE, 1, sides.at[pl.ds(NW, 1)], 3, (east, south), has_south, 1),
         (TO_NORTH, 9, rows_in.at[SOUTH + top], SOUTH + top, north(bx), None, top),
-        (TO_NE, 1, sides.at[pl.ds(SW + (NE - SW) * top, 1)], 2, ne_to, ne_other, 1),
+        (TO_NE, 1, sides.at[pl.ds(SW + (NE - SW) * top, 1)], 3, ne_to, ne_other, 1),
         (TO_WEST, 3, sides.at[pl.ds(EAST, 3)], 2, (west, by), None, 0),
-        (TO_SW, 1, sides.at[pl.ds(NE, 1)], 2, (west, south), has_south, 0),
-        (TO_NW, 1, sides.at[pl.ds(SE + (NW - SE) * top, 1)], 2, nw_to, nw_other, top),
+        (TO_SW, 1, sides.at[pl.ds(NE, 1)], 3, (west, south), has_south, 0),
+        (TO_NW, 1, sides.at[pl.ds(SE + (NW - SE) * top, 1)], 3, nw_to, nw_other, top),
     ]
     groups = (0, 0, 0, top, top, 1, 1, 1)
 
     stranger_south = jnp.logical_and(bx == nb - 1, by % 2 == 0)
     stranger_north = jnp.logical_and(jnp.logical_and(bx == nb - 1, by % 2 == 1), by < ny - 1)
     introduces = jnp.logical_and(jnp.logical_and(bx == 0, by % 2 == 1), by < ny - 1)
+    lowest = max(nb - 4, nb // 2)
+    stranger_east = jnp.logical_and(top == 1, jnp.logical_and(bx >= lowest, bx < nb - 1))
+    stranger_west = jnp.logical_and(top == 1, bx > lowest)
+    introduces_folded = jnp.logical_and(top == 1, jnp.logical_and(bx >= 1, bx < nb - lowest))
+    strangers = {0: stranger_south, 3: stranger_north, 1: stranger_east, 5: stranger_west}
     before, after, greets = [], [], []
     for i, (_, _, _, _, device, condition, _) in enumerate(plan):
         earlier = is_earlier(*device)
-        if i in (0, 3):
-            stranger = stranger_south if i == 0 else stranger_north
-            earlier = jnp.logical_and(earlier, jnp.logical_not(stranger))
+        if i in strangers:
+            earlier = jnp.logical_and(earlier, jnp.logical_not(strangers[i]))
         later = jnp.logical_not(earlier)
         before.append(earlier if condition is None else jnp.logical_and(condition, earlier))
         after.append(later if condition is None else jnp.logical_and(condition, later))
-        greets.append(jnp.logical_and(after[i], jnp.logical_not(stranger)) if i in (0, 3) else after[i])
+        greets.append(jnp.logical_and(after[i], jnp.logical_not(strangers[i])) if i in strangers else after[i])
 
     def signal(semaphore, device):
         pl.semaphore_signal(semaphore, inc=1, device_id=device, device_id_type=MESH)
@@ -214,26 +219,26 @@
 
     loads[0].wait()
     pltpu.make_async_copy(tips, tips, load_sem.at[3]).wait()
-    depth[...] = depth_i[...].astype(jnp.float32)
-
-    def corner_cells(i, r):
+    def corner_cells(i, r, shift, at):
         value = jnp.zeros((LEV, CX), jnp.float32)
         for f in range(FIELDS + 1):
             if f < FIELDS:
                 line = tips[pl.ds((i * FIELDS + f) * LEV, LEV), :]
             else:
-                line = jnp.broadcast_to(depth[pl.ds(r, 1), :], (LEV, CX))
-            value = jnp.where((lane + 1) // 4 == f + 2, pltpu.roll(line, BASE + 4 * f, 1), value)
+                line = jnp.broadcast_to(depth_i[pl.ds(r, 1), :].astype(jnp.float32), (LEV, CX))
+            value = jnp.where((lane - at) // 4 == f, pltpu.roll(line, shift + 4 * f, 1), value)
         return value
 
-    upper, lower = corner_cells(0, CY - 1), corner_cells(1, 0)
+    sent[TO_SE] = corner_cells(1, 0, 33 + BASE, 32 + BASE)
+    send_to_earlier(2)
+    sent[TO_SW] = corner_cells(1, 0, 96 + BASE, 96 + BASE)
+    upper = corner_cells(0, CY - 1, BASE, BASE - 1)
     upper = upper * jnp.where((lane + 1) // 8 == 2, flip, 1.0)
     sent[TO_NE] = jnp.where(left, upper, pltpu.roll(upper, 97, 1))
     sent[TO_NW] = jnp.where(left, pltpu.roll(upper, 32, 1), pltpu.roll(upper, 63, 1))
-    sent[TO_SE] = pltpu.roll(lower, 33, 1)
-    sent[TO_SW] = pltpu.roll(lower, 96, 1)
-    send_to_earlier(4, 2, 7, 6)
-
+    send_to_earlier(4, 7, 6)
+
+    depth[...] = depth_i[...].astype(jnp.float32)
     for load in loads[1:]:
         load.wait()
     for side, rows in ((TO_NORTH, (31, 30)), (TO_SOUTH, (0, 1))):
@@ -250,6 +255,8 @@
             mirrored = jnp.take_along_axis(sent[TO_NORTH + i], (CX - 1) - lane, axis=1)
             sent[TO_NORTH + i] = -mirrored if i in (4, 5, 6, 7) else mirrored
 
+        pl.when(jnp.logical_and(before[3], bx == nb - 1))(copies[3].start)
+
     def transposed(group, value):
         tall[group, pl.ds(BASE, CY), :] = value
         tall[group, pl.ds(64 + BASE, CY), :] = value
@@ -277,7 +284,8 @@
     side_columns(TO_EAST, 3, 2)
     side_columns(TO_WEST, 5, 4)
     send_to_earlier(1, 5)
-    send_to_earlier(3, 0)
+    pl.when(jnp.logical_and(before[3], jnp.logical_or(top == 0, bx < nb - 1)))(copies[3].start)
+    send_to_earlier(0)
 
     @pl.when(jnp.logical_not(ne_other))
     def _():
@@ -305,6 +313,11 @@
     def _():
         signal(go_sem.at[0], (west, by))
         signal(go_sem.at[0], (west, by + 1))
+
+    @pl.when(introduces_folded)
+    def _():
+        signal(go_sem.at[0], north(bx))
+        signal(go_sem.at[1], nw_to)
 
     def wait_received(ref, slot):
         pltpu.make_async_remote_copy(
@@ -363,17 +376,7 @@
     next_one = Line(lines[1].step(lines[2], lines[0], 3, sign), depths[1], planetary)
     next_two = Line(lines[2].step(lines[3], lines[1], 3, sign), depths[2], whole=False)
 
-    all_other = jnp.logical_and(ne_other, nw_other)
-    for condition, tiles in (
-        (jnp.logical_and(has_south, all_other), SIDES),
-        (jnp.logical_not(has_south), SIDES - 2),
-        (jnp.logical_not(all_other), SIDES - 1),
-    ):
-        pl.when(condition)(functools.partial(wait_received, sides.at[pl.ds(0, tiles)], 2))
-
-    corner = jnp.where(
-        left, jnp.where(lane < 32, sides[SW], sides[NW]), jnp.where(lane < 96, sides[SE], sides[NE]))
-    at_corner = jnp.logical_or(lane % 64 == BASE - 1, lane % 64 == BASE + CY)
+    wait_received(sides.at[pl.ds(0, SW)], 2)
 
     def outside(f):
         shift = CY if f in (1, 3) else 0
@@ -383,14 +386,17 @@
         far = jnp.where(west_lanes, east_tile, west_tile)
         if shift:
             near = pltpu.roll(near, CX - shift, 1)
-        shifted = corner if f == 0 else pltpu.roll(corner, CX - 4 * f, 1)
-        return jnp.where(at_corner, shifted, near), pltpu.roll(far, 64 - shift, 1)
+        return near, pltpu.roll(far, 64 - shift, 1)
 
     beyond = [outside(f) for f in range(FIELDS + 1)]
     far = Line([beyond[f][1] for f in range(FIELDS)], beyond[FIELDS][1], whole=False)
-    near = Line([beyond[f][0] for f in range(FIELDS)], beyond[FIELDS][0], planetary)
-    next_near = Line(near.step(lines[0], far, 3, sign), beyond[FIELDS][0], whole=False)
-    next_zero = Line(lines[0].step(lines[1], near, 3, sign), depths[0], planetary)
+
+    def first_step(values):
+        near = Line(values[:FIELDS], values[FIELDS], planetary)
+        next_near = Line(near.step(lines[0], far, 3, sign), values[FIELDS], whole=False)
+        return next_near, Line(lines[0].step(lines[1], near, 3, sign), depths[0], planetary)
+
+    next_near, next_zero = first_step([near for near, _ in beyond])
     second = (next_zero.step(next_one, next_near, 3, sign), next_one.step(next_two, next_zero, 3, sign))
 
     for f in range(FIELDS):
@@ -403,6 +409,7 @@
         spot = out.at[pl.ds(p * CY, CY)]
         spot[...] = jnp.where(at_edge, pltpu.roll(edges, (126 - 4 * p) % CX, 1), spot[...])
 
+    all_other = jnp.logical_and(ne_other, nw_other)
     def wait_sent(tiles):
         ref = sent.at[pl.ds(0, tiles)]
         pltpu.make_async_remote_copy(
@@ -415,6 +422,28 @@
         (jnp.logical_not(all_other), SENT - 1),
     ):
         pl.when(condition)(functools.partial(wait_sent, tiles))
+
+    for condition, tiles in (
+        (jnp.logical_and(has_south, all_other), SIDES - SW),
+        (jnp.logical_not(has_south), SIDES - SW - 2),
+        (jnp.logical_not(all_other), SIDES - SW - 1),
+    ):
+        pl.when(condition)(functools.partial(wait_received, sides.at[pl.ds(SW, tiles)], 3))
+
+    corner = jnp.where(
+        left, jnp.where(lane < 32, sides[SW], sides[NW]), jnp.where(lane < 96, sides[SE], sides[NE]))
+    at_corner = jnp.logical_or(lane % 64 == BASE - 1, lane % 64 == BASE + CY)
+    next_near, next_zero = first_step([
+        jnp.where(at_corner, corner if f == 0 else pltpu.roll(corner, CX - 4 * f, 1), near)
+        for f, (near, _) in enumerate(beyond)
+    ])
+    final = next_zero.step(next_one, next_near, 3, sign)
+    for f in range(FIELDS):
+        for r in (0, CY - 1):
+            spot = out.at[pl.ds(f * LEV * CY + r, LEV, stride=CY), :]
+            spot[...] = jnp.where(
+                lane == 0, pltpu.roll(final[f], CX - BASE - r, 1),
+                jnp.where(lane == CX - 1, pltpu.roll(final[f], 63 - BASE - r, 1), spot[...]))
 
 
 def local(nb, ny, state, level_count, coriolis):
@@ -440,7 +469,7 @@
             vmem((2, 9, LEV, CX), f32),
             pltpu.SemaphoreType.DMA((4,)),
             pltpu.SemaphoreType.DMA,
-            pltpu.SemaphoreType.DMA((3,)),
+            pltpu.SemaphoreType.DMA((4,)),
             pltpu.SemaphoreType.REGULAR((2,)),
         ],
         compiler_params=pltpu.CompilerParams(collective_id=0, has_side_effects=True),

time: 17.2 us -> 16.9 us (0.983)
  Pallas kernels: 16.3 us -> 16 us
    pallas_call x1, Pallas kernels: 16.3 us -> 16 us  [local(): pl.pallas_call(functools.partial(kernel, nb, ny), out_shape=vmem((FIELDS...]
where the time goes in v5:
time: 16.9 us; the launch traced here: 16.8 us
  Pallas kernels  16 us (95%)
  local copies, waits for them, and re-layouts  0.8 us (5%)
    pallas_call x1, Pallas kernels, local(): pl.pallas_call(functools.partial(kernel, nb, ny), out_shape=vmem((FIELDS...  16 us
    unnamed x1, local copies, waits for them, and re-layouts  0.8 us

profile of v5, /device:TPU:1, one launch (start us, length us, event | category | flops | bytes accessed | tf_op | source)
XLA Modules:
  0.0 16.8 jit_solution(14045709716225581747)
XLA Ops:
  0.0 16.0 %shard_map.37 = f32[1024,128]{1,0:T(8,128)S(1)} custom-call(f32[1024,128]{1,0:T(8,128)} %bitcast.4, f32[32,32,128]{2,1,0:T(8,128)} %bitcast.5, s32[32,128]{1,0:T(8,128)} %level_count.1, f32[32]{0:T(128)} %coriolis.1), custom_call_target="tpu_custom_call" | custom-call | tf_op jit(solution)/shard_map/pallas_call | solution.py:452
  16.0 0.8 %copy.5 = f32[4,8,32,128]{3,2,1,0:T(8,128)} copy(f32[4,8,32,128]{3,2,1,0:T(8,128)S(1)} %bitcast.3) | data formatting | bytes 1048576

commit v6 on v5

--- a/solution.py
+++ b/solution.py
@@ -1,3 +1,4 @@
+import copy
 import functools
 
 import jax
@@ -60,6 +61,14 @@
                 for shift in (CX - 1, 1)
             ]
 
+    def mixed(self, there, other):
+        line = copy.copy(self)
+        line.fields = [jnp.where(there, b, a) for a, b in zip(self.fields, other.fields)]
+        line.mask = jnp.logical_or(
+            jnp.logical_and(there, other.mask), jnp.logical_and(jnp.logical_not(there), self.mask))
+        line.pressure = jnp.where(there, other.pressure, self.pressure)
+        return line
+
     def step(self, inner, outer, along, sign_across):
         (ahead, m_a, p_a), (behind, m_b, p_b) = self.around
         return update(
@@ -99,8 +108,8 @@
 ):
     bx, by = lax.axis_index("bx"), lax.axis_index("by")
     tip_loads = [
-        pltpu.make_async_copy(planes.at[:, r, :], tips.at[pl.ds(i * FIELDS * LEV, FIELDS * LEV)], load_sem.at[3])
-        for i, r in enumerate((CY - 1, 0))
+        pltpu.make_async_copy(planes.at[:, r, :], tips.at[pl.ds(i * FIELDS * LEV, FIELDS * LEV)], load_sem.at[3 + i])
+        for i, r in ((1, 0), (0, CY - 1))
     ]
     loads = [
         pltpu.make_async_copy(level_count, depth_i, load_sem.at[1]),
@@ -190,8 +199,6 @@
         answers[0] = answers[0] + counted * (1 - groups[i])
         answers[1] = answers[1] + counted * groups[i]
     pl.when(greetings > 0)(functools.partial(pl.semaphore_wait, barrier, greetings))
-    for i, (_, _, _, _, device, _, group) in enumerate(plan):
-        pl.when(before[i])(functools.partial(signal, go_sem.at[group], device))
     copies = [
         pltpu.make_async_remote_copy(
             src_ref=sent.at[pl.ds(first, tiles)], dst_ref=target, send_sem=send_sem, recv_sem=recv_sem.at[slot],
@@ -218,24 +225,29 @@
         return ref[pl.ds(f * LEV * CY + r, LEV, stride=CY), :]
 
     loads[0].wait()
-    pltpu.make_async_copy(tips, tips, load_sem.at[3]).wait()
-    def corner_cells(i, r, shift, at):
+    tip_loads[0].wait()
+    def corner_cells(i, r, c, places, scale=None):
         value = jnp.zeros((LEV, CX), jnp.float32)
         for f in range(FIELDS + 1):
             if f < FIELDS:
-                line = tips[pl.ds((i * FIELDS + f) * LEV, LEV), :]
+                line = tips[pl.ds((i * FIELDS + f) * LEV, LEV), c : c + 1]
             else:
-                line = jnp.broadcast_to(depth_i[pl.ds(r, 1), :].astype(jnp.float32), (LEV, CX))
-            value = jnp.where((lane - at) // 4 == f, pltpu.roll(line, shift + 4 * f, 1), value)
+                line = jnp.broadcast_to(depth_i[pl.ds(r, 1), c : c + 1].astype(jnp.float32), (LEV, 1))
+            if scale is not None and f in (2, 3):
+                line = line * scale
+            there = functools.reduce(
+                jnp.logical_or, [jnp.logical_and(lane >= at + 4 * f, lane < at + 4 * f + 4) for at in places])
+            value = jnp.where(there, line, value)
         return value
 
-    sent[TO_SE] = corner_cells(1, 0, 33 + BASE, 32 + BASE)
+    sent[TO_SE] = corner_cells(1, 0, CX - 1, (31 + BASE,))
     send_to_earlier(2)
-    sent[TO_SW] = corner_cells(1, 0, 96 + BASE, 96 + BASE)
-    upper = corner_cells(0, CY - 1, BASE, BASE - 1)
-    upper = upper * jnp.where((lane + 1) // 8 == 2, flip, 1.0)
-    sent[TO_NE] = jnp.where(left, upper, pltpu.roll(upper, 97, 1))
-    sent[TO_NW] = jnp.where(left, pltpu.roll(upper, 32, 1), pltpu.roll(upper, 63, 1))
+    for i, (_, _, _, _, device, _, group) in enumerate(plan):
+        pl.when(before[i])(functools.partial(signal, go_sem.at[group], device))
+    sent[TO_SW] = corner_cells(1, 0, 0, (95 + BASE,))
+    tip_loads[1].wait()
+    sent[TO_NE] = corner_cells(0, CY - 1, CX - 1, (BASE - 2, 95 + BASE), flip)
+    sent[TO_NW] = corner_cells(0, CY - 1, 0, (62 + BASE, 31 + BASE), flip)
     send_to_earlier(4, 7, 6)
 
     depth[...] = depth_i[...].astype(jnp.float32)
@@ -300,7 +312,7 @@
     block_step(x, y, depth[...], turn[...])
     block_step(y, out, depth[...], turn[...])
 
-    for group in range(2):
+    def exchange(group):
         pl.when(answers[group] > 0)(functools.partial(pl.semaphore_wait, go_sem.at[group], answers[group]))
         for i in range(8):
             if isinstance(groups[i], int):
@@ -309,15 +321,17 @@
             else:
                 pl.when(jnp.logical_and(after[i], groups[i] == group))(copies[i].start)
 
-    @pl.when(introduces)
+    first_column = jnp.logical_and(bx == 0, top == 0)
+    exchange(0)
+
+    @pl.when(jnp.logical_not(first_column))
     def _():
-        signal(go_sem.at[0], (west, by))
-        signal(go_sem.at[0], (west, by + 1))
-
-    @pl.when(introduces_folded)
-    def _():
-        signal(go_sem.at[0], north(bx))
-        signal(go_sem.at[1], nw_to)
+        exchange(1)
+
+        @pl.when(introduces_folded)
+        def _():
+            signal(go_sem.at[0], north(bx))
+            signal(go_sem.at[1], nw_to)
 
     def wait_received(ref, slot):
         pltpu.make_async_remote_copy(
@@ -376,6 +390,15 @@
     next_one = Line(lines[1].step(lines[2], lines[0], 3, sign), depths[1], planetary)
     next_two = Line(lines[2].step(lines[3], lines[1], 3, sign), depths[2], whole=False)
 
+    @pl.when(first_column)
+    def _():
+        exchange(1)
+
+        @pl.when(introduces)
+        def _():
+            signal(go_sem.at[0], (west, by))
+            signal(go_sem.at[0], (west, by + 1))
+
     wait_received(sides.at[pl.ds(0, SW)], 2)
 
     def outside(f):
@@ -391,12 +414,13 @@
     beyond = [outside(f) for f in range(FIELDS + 1)]
     far = Line([beyond[f][1] for f in range(FIELDS)], beyond[FIELDS][1], whole=False)
 
-    def first_step(values):
-        near = Line(values[:FIELDS], values[FIELDS], planetary)
-        next_near = Line(near.step(lines[0], far, 3, sign), values[FIELDS], whole=False)
+    def first_step(near, at_center=None):
+        next_near = Line(near.step(lines[0], far, 3, sign), beyond[FIELDS][0], whole=False)
+        near = at_center or near
         return next_near, Line(lines[0].step(lines[1], near, 3, sign), depths[0], planetary)
 
-    next_near, next_zero = first_step([near for near, _ in beyond])
+    near = Line([value for value, _ in beyond[:FIELDS]], beyond[FIELDS][0], planetary)
+    next_near, next_zero = first_step(near)
     second = (next_zero.step(next_one, next_near, 3, sign), next_one.step(next_two, next_zero, 3, sign))
 
     for f in range(FIELDS):
@@ -432,11 +456,17 @@
 
     corner = jnp.where(
         left, jnp.where(lane < 32, sides[SW], sides[NW]), jnp.where(lane < 96, sides[SE], sides[NE]))
+    cells = [corner if f == 0 else pltpu.roll(corner, CX - 4 * f, 1) for f in range(FIELDS + 1)]
+    beside = Line(cells[:FIELDS], cells[FIELDS], whole=False)
     at_corner = jnp.logical_or(lane % 64 == BASE - 1, lane % 64 == BASE + CY)
-    next_near, next_zero = first_step([
-        jnp.where(at_corner, corner if f == 0 else pltpu.roll(corner, CX - 4 * f, 1), near)
-        for f, (near, _) in enumerate(beyond)
-    ])
+    with_corner = copy.copy(near)
+    with_corner.around = []
+    for (fields, mask, pressure), r in zip(near.around, (CY - 1, 0)):
+        side = copy.copy(near)
+        side.fields, side.mask, side.pressure = fields, mask, pressure
+        side = side.mixed(lane % 64 == BASE + r, beside)
+        with_corner.around.append((side.fields, side.mask, side.pressure))
+    next_near, next_zero = first_step(with_corner, near.mixed(at_corner, beside))
     final = next_zero.step(next_one, next_near, 3, sign)
     for f in range(FIELDS):
         for r in (0, CY - 1):
@@ -467,7 +497,7 @@
             vmem((SENT, LEV, CX), f32),
             vmem((SIDES, LEV, CX), f32),
             vmem((2, 9, LEV, CX), f32),
-            pltpu.SemaphoreType.DMA((4,)),
+            pltpu.SemaphoreType.DMA((5,)),
             pltpu.SemaphoreType.DMA,
             pltpu.SemaphoreType.DMA((4,)),
             pltpu.SemaphoreType.REGULAR((2,)),

time: 16.9 us -> 17 us (level)
  no operation moved by 1% of the time
where the time goes in v6:
time: 17 us; the launch traced here: 16.8 us
  Pallas kernels  16 us (94%)
  local copies, waits for them, and re-layouts  0.8 us (5%)
    pallas_call x1, Pallas kernels, local(): pl.pallas_call(functools.partial(kernel, nb, ny), out_shape=vmem((FIELDS...  16 us
    unnamed x1, local copies, waits for them, and re-layouts  0.8 us

profile of v6, /device:TPU:1, one launch (start us, length us, event | category | flops | bytes accessed | tf_op | source)
XLA Modules:
  0.0 16.8 jit_solution(17926212192074780778)
XLA Ops:
  0.0 16.0 %shard_map.37 = f32[1024,128]{1,0:T(8,128)S(1)} custom-call(f32[1024,128]{1,0:T(8,128)} %bitcast.4, f32[32,32,128]{2,1,0:T(8,128)} %bitcast.5, s32[32,128]{1,0:T(8,128)} %level_count.1, f32[32]{0:T(128)} %coriolis.1), custom_call_target="tpu_custom_call" | custom-call | tf_op jit(solution)/shard_map/pallas_call | solution.py:482
  16.0 0.8 %copy.5 = f32[4,8,32,128]{3,2,1,0:T(8,128)} copy(f32[4,8,32,128]{3,2,1,0:T(8,128)S(1)} %bitcast.3) | data formatting | bytes 1048576

commit v7 on v6

--- a/solution.py
+++ b/solution.py
@@ -116,7 +116,7 @@
         pltpu.make_async_copy(state, x, load_sem.at[0]),
         pltpu.make_async_copy(coriolis, turn_s, load_sem.at[2]),
     ]
-    for load in tip_loads + loads:
+    for load in (tip_loads[0], loads[0], tip_loads[1], *loads[1:]):
         load.start()
 
     top = by // (ny - 1)

time: 17 us -> 17 us (level)
  no operation moved by 1% of the time
where the time goes in v7:
time: 17 us; the launch traced here: 16.8 us
  Pallas kernels  16 us (94%)
  local copies, waits for them, and re-layouts  0.8 us (5%)
    pallas_call x1, Pallas kernels, local(): pl.pallas_call(functools.partial(kernel, nb, ny), out_shape=vmem((FIELDS...  16 us
    unnamed x1, local copies, waits for them, and re-layouts  0.8 us

profile of v7, /device:TPU:1, one launch (start us, length us, event | category | flops | bytes accessed | tf_op | source)
XLA Modules:
  0.0 16.8 jit_solution(1501537895293745221)
XLA Ops:
  0.0 16.0 %shard_map.37 = f32[1024,128]{1,0:T(8,128)S(1)} custom-call(f32[1024,128]{1,0:T(8,128)} %bitcast.4, f32[32,32,128]{2,1,0:T(8,128)} %bitcast.5, s32[32,128]{1,0:T(8,128)} %level_count.1, f32[32]{0:T(128)} %coriolis.1), custom_call_target="tpu_custom_call" | custom-call | tf_op jit(solution)/shard_map/pallas_call | solution.py:482
  16.0 0.8 %copy.5 = f32[4,8,32,128]{3,2,1,0:T(8,128)} copy(f32[4,8,32,128]{3,2,1,0:T(8,128)S(1)} %bitcast.3) | data formatting | bytes 1048576

commit v8 on v7

--- a/solution.py
+++ b/solution.py
@@ -199,6 +199,8 @@
         answers[0] = answers[0] + counted * (1 - groups[i])
         answers[1] = answers[1] + counted * groups[i]
     pl.when(greetings > 0)(functools.partial(pl.semaphore_wait, barrier, greetings))
+    for i, (_, _, _, _, device, _, group) in enumerate(plan):
+        pl.when(before[i])(functools.partial(signal, go_sem.at[group], device))
     copies = [
         pltpu.make_async_remote_copy(
             src_ref=sent.at[pl.ds(first, tiles)], dst_ref=target, send_sem=send_sem, recv_sem=recv_sem.at[slot],
@@ -242,8 +244,6 @@
 
     sent[TO_SE] = corner_cells(1, 0, CX - 1, (31 + BASE,))
     send_to_earlier(2)
-    for i, (_, _, _, _, device, _, group) in enumerate(plan):
-        pl.when(before[i])(functools.partial(signal, go_sem.at[group], device))
     sent[TO_SW] = corner_cells(1, 0, 0, (95 + BASE,))
     tip_loads[1].wait()
     sent[TO_NE] = corner_cells(0, CY - 1, CX - 1, (BASE - 2, 95 + BASE), flip)

time: 17 us -> 17 us (level)
  no operation moved by 1% of the time
where the time goes in v8:
time: 17 us; the launch traced here: 16.8 us
  Pallas kernels  16 us (94%)
  local copies, waits for them, and re-layouts  0.8 us (5%)
    pallas_call x1, Pallas kernels, local(): pl.pallas_call(functools.partial(kernel, nb, ny), out_shape=vmem((FIELDS...  16 us
    unnamed x1, local copies, waits for them, and re-layouts  0.8 us

profile of v8, /device:TPU:1, one launch (start us, length us, event | category | flops | bytes accessed | tf_op | source)
XLA Modules:
  0.0 16.8 jit_solution(18248448432100469203)
XLA Ops:
  0.0 16.0 %shard_map.37 = f32[1024,128]{1,0:T(8,128)S(1)} custom-call(f32[1024,128]{1,0:T(8,128)} %bitcast.4, f32[32,32,128]{2,1,0:T(8,128)} %bitcast.5, s32[32,128]{1,0:T(8,128)} %level_count.1, f32[32]{0:T(128)} %coriolis.1), custom_call_target="tpu_custom_call" | custom-call | tf_op jit(solution)/shard_map/pallas_call | solution.py:482
  16.0 0.8 %copy.5 = f32[4,8,32,128]{3,2,1,0:T(8,128)} copy(f32[4,8,32,128]{3,2,1,0:T(8,128)S(1)} %bitcast.3) | data formatting | bytes 1048576
